TPU v7x, 128 devices: a whole 4x4x4 slice. The times are simulated.
128 devices in a mesh: dp: 2 (over core), expert: 64 (over z, x, y).
Axes of the slice: x: 4, y: 4, z: 4, core: 2. Of those that a mesh axis runs over, the one named last changes fastest.
Arguments:
- tokens: bfloat16 [16384, 2048], P(('dp', 'expert')), may hold values from -6 to 6
- cotangent: bfloat16 [16384, 2048], P(('dp', 'expert')), may hold values from -6 to 6
- routes: int32 [16384, 8], P(('dp', 'expert')), may hold values from 0 to 63, all different within a row
- route_weight: int32 [16384, 8], P(('dp', 'expert')), may hold values from 1 to 4096
- replica_pick: int32 [16384, 8], P(('dp', 'expert')), may hold values 0 or 1
- hot_experts: int32 [8], replicated, may hold values from 0 to 63, as said below
- hot_holders: int32 [8], replicated, may hold values from 1 to 62, as said below
- capacity: int32 [64], replicated, may hold values from 6 to 8
- gate_weight: bfloat16 [64, 2048, 768], P('expert'), may hold values from -0.125 to 0.125
- up_weight: bfloat16 [64, 2048, 768], P('expert'), may hold values from -0.125 to 0.125
- down_weight: bfloat16 [64, 2048, 768], P('expert'), may hold values from -0.21875 to 0.21875
Outputs:
- mixed: bfloat16 [16384, 2048], P(('dp', 'expert'))
- grad_tokens: bfloat16 [16384, 2048], P(('dp', 'expert'))
- grad_gate: bfloat16 [64, 2048, 768], P('expert', 'dp')
- grad_up: bfloat16 [64, 2048, 768], P('expert', 'dp')
- grad_down: bfloat16 [64, 2048, 768], P('expert', 'dp')
Inputs may be any that keep to these rules, and one draw needn't show every extreme that they name: `hot_experts`: 8 distinct experts. 8 distinct indices along expert, none of them equal to an entry of hot_experts; the device at hot_holders[j] holds the replica of hot_experts[j].
All inputs are finite; a program needn't handle non-finite values. No bound on the sum of `replica_pick` on one device may be relied on, other than what follows from the above.
Results may differ from a plain program's by a relative error of at most 0.0095.
Values may be sent and summed in bfloat16 or wider, within the bound.
No kernel may reach another device: no remote copies, remote signals or barrier semaphores. Data moves between devices by JAX's collectives and lax.ppermute only.
A program may use at most 192 MiB of HBM per device.

v0:
```python
import jax
import jax.numpy as jnp
from jax import lax
from jax.experimental import pallas as pl
from jax.experimental.pallas import tpu as pltpu
from jax.sharding import PartitionSpec as P

D = 2048
FF = 768
TOPK = 8
HOT = 8
CAP = 8
RCAP = 3
TOK = 128
EXPERTS = 64
HOME = EXPERTS * CAP
FAR = EXPERTS * RCAP
PARTS = 8
PIECE = D // PARTS
WIDE = D + RCAP * PIECE
STEP = 256
BF = jnp.bfloat16
F32 = jnp.float32
VMEM_LIMIT = 56 * 1024 * 1024


def dot(a, b, dims=((1,), (0,))):
    return lax.dot_general(a, b, (dims, ((), ())), preferred_element_type=F32)


def fold_matrix(transposed):
    row = lax.broadcasted_iota(jnp.int32, (HOME, HOME), 0)
    col = lax.broadcasted_iota(jnp.int32, (HOME, HOME), 1)
    if transposed:
        row, col = col, row
    return (col == (row % EXPERTS) * PARTS + row // EXPERTS).astype(F32).astype(BF)


def unfold(folded, rows_ref):
    flat = dot(fold_matrix(False), folded).astype(BF)
    for i in range(PARTS):
        for f in range(RCAP):
            rows_ref[f * EXPERTS:(f + 1) * EXPERTS, i * PIECE:(i + 1) * PIECE] = flat[
                i * EXPERTS:(i + 1) * EXPERTS, f * PIECE:(f + 1) * PIECE
            ]


def fold(rows):
    flat = jnp.concatenate(
        [
            jnp.concatenate(
                [
                    rows[f * EXPERTS:(f + 1) * EXPERTS, i * PIECE:(i + 1) * PIECE]
                    for f in range(RCAP)
                ],
                axis=1,
            )
            for i in range(PARTS)
        ],
        axis=0,
    )
    return dot(fold_matrix(True), flat).astype(BF)


def picks(slots, scale=None):
    home_slots, far_slots = slots[:EXPERTS], slots[EXPERTS:]
    s = lax.broadcasted_iota(jnp.int32, (EXPERTS, CAP, TOK), 1).astype(F32) + 1.0
    home_value = F32(1.0) if scale is None else scale[:EXPERTS][:, None, :]
    home = jnp.where(home_slots[:, None, :] == s, home_value, 0.0).reshape(HOME, TOK)
    far_value = F32(1.0) if scale is None else scale[EXPERTS:]
    far = jnp.concatenate(
        [jnp.where(far_slots == F32(f + 1), far_value, 0.0) for f in range(RCAP)], axis=0
    )
    return home, far


def plan_kernel(hot_ref, holder_ref, cap_ref, routes_ref, weight_ref, pick_ref, tokens_ref,
                send_ref, slots_ref, scale_ref):
    lane = lax.broadcasted_iota(jnp.int32, (1, TOK), 1)
    expert = lane % EXPERTS
    far_lane = lane >= EXPERTS
    limit = jnp.zeros((1, TOK), jnp.int32)
    for e in range(EXPERTS):
        limit = jnp.where(lane == e, cap_ref[e], limit)
    hot = jnp.zeros((1, TOK), jnp.int32)
    for j in range(HOT):
        here = expert == hot_ref[j]
        hot = jnp.where(here, 1, hot)
        limit = jnp.where(
            jnp.logical_and(here, far_lane), jnp.minimum(cap_ref[holder_ref[j]], RCAP), limit
        )
    far_value = jnp.where(far_lane, 1, 0)
    present = jnp.zeros((TOK, TOK), F32)
    scale = jnp.zeros((TOK, TOK), F32)
    for k in range(TOPK):
        replica = hot * pick_ref[:, k:k + 1]
        match = jnp.logical_and(routes_ref[:, k:k + 1] == expert, replica == far_value)
        present = jnp.where(match, 1.0, present)
        scale = jnp.where(match, weight_ref[:, k:k + 1].astype(F32), scale)
    row = lax.broadcasted_iota(jnp.int32, (TOK, TOK), 0)
    col = lax.broadcasted_iota(jnp.int32, (TOK, TOK), 1)
    before = (col < row).astype(F32).astype(BF)
    same = (col == row).astype(F32).astype(BF)
    rank = dot(before, present.astype(BF))
    kept = jnp.logical_and(present > 0.0, rank < limit.astype(F32))
    slots = jnp.where(kept, rank + 1.0, 0.0).astype(BF)
    high = scale.astype(BF)
    low = (scale - high.astype(F32)).astype(BF)
    turn = ((0,), (0,))
    slots = dot(slots, same, turn)
    slots_ref[...] = slots
    scale_ref[...] = (dot(high, same, turn) + dot(low, same, turn)) * (1.0 / 4096.0)
    home, far = picks(slots)
    home, far = home.astype(BF), far.astype(BF)
    for c in range(0, D, STEP):
        send_ref[:, c:c + STEP] = dot(home, tokens_ref[:, c:c + STEP]).astype(BF)
    send_ref[:, D:] = fold(dot(far, tokens_ref[...]).astype(BF))


def split(values):
    high = values.astype(BF)
    return high, (values - high.astype(F32)).astype(BF)


def grads_kernel(slots_ref, scale_ref, cot_ref, send_ref):
    home, far = picks(slots_ref[...], scale_ref[...])
    home = jnp.concatenate(split(home), axis=1)
    far = jnp.concatenate(split(far), axis=1)
    for c in range(0, D, STEP):
        cot = cot_ref[:, c:c + STEP]
        send_ref[:, c:c + STEP] = dot(home, jnp.concatenate([cot, cot], axis=0)).astype(BF)
    cot = cot_ref[...]
    send_ref[:, D:] = fold(dot(far, jnp.concatenate([cot, cot], axis=0)).astype(BF))


def forward_kernel(got_ref, gate_ref, up_ref, down_ref,
                   send_ref, far_ref, hidden_ref, gate_factor_ref, up_factor_ref):
    unfold(got_ref[:, D:], far_ref)

    def hidden_step(n, carry):
        cols = pl.ds(pl.multiple_of(n * STEP, STEP), STEP)
        for first, rows in ((0, got_ref), (HOME, far_ref)):
            x = rows[:, :D]
            count = x.shape[0]
            pre_gate = dot(x, gate_ref[:, cols])
            pre_up = dot(x, up_ref[:, cols])
            sigma = jax.nn.sigmoid(pre_gate)
            active = pre_gate * sigma
            hidden_ref[first:first + count, cols] = (active * pre_up).astype(BF)
            gate_factor_ref[first:first + count, cols] = (
                pre_up * sigma * (1.0 + pre_gate * (1.0 - sigma))
            )
            up_factor_ref[first:first + count, cols] = active
        return carry

    lax.fori_loop(0, FF // STEP, hidden_step, 0)
    outputs(send_ref, [(hidden_ref, down_ref)])


def outputs(send_ref, pairs):
    def out_step(n, carry):
        cols = pl.ds(pl.multiple_of(n * PIECE, PIECE), PIECE)
        total = sum(dot(rows[:HOME], w[cols, :], ((1,), (1,))) for rows, w in pairs)
        send_ref[:, cols] = total.astype(BF)
        return carry

    lax.fori_loop(0, PARTS, out_step, 0)
    far = sum(dot(rows[HOME:], w[...], ((1,), (1,))) for rows, w in pairs)
    send_ref[:, D:] = fold(far.astype(BF))


def backward_kernel(got_ref, gate_ref, up_ref, down_ref, gate_factor_ref, up_factor_ref,
                    send_ref, far_ref, back_gate_ref, back_up_ref):
    unfold(got_ref[:, D:], far_ref)

    def hidden_step(n, carry):
        cols = pl.ds(pl.multiple_of(n * STEP, STEP), STEP)
        for first, rows in ((0, got_ref), (HOME, far_ref)):
            g = rows[:, :D]
            count = g.shape[0]
            back_hidden = dot(g, down_ref[:, cols])
            here = slice(first, first + count)
            back_gate_ref[here, cols] = (back_hidden * gate_factor_ref[here, cols]).astype(BF)
            back_up_ref[here, cols] = (back_hidden * up_factor_ref[here, cols]).astype(BF)
        return carry

    lax.fori_loop(0, FF // STEP, hidden_step, 0)
    outputs(send_ref, [(back_gate_ref, gate_ref), (back_up_ref, up_ref)])


def weight_kernel(home_ref, far_ref, *refs):
    count = len(refs) // 2

    def step(n, carry):
        cols = pl.ds(pl.multiple_of(n * STEP, STEP), STEP)
        home, far = home_ref[:, cols], far_ref[:, cols]
        for back, grad in zip(refs[:count], refs[count:]):
            turn = ((0,), (0,))
            grad[cols, :] = (dot(home, back[:HOME], turn) + dot(far, back[HOME:], turn)).astype(BF)
        return carry

    lax.fori_loop(0, D // STEP, step, 0)


def mixed_kernel(slots_ref, scale_ref, got_ref, mixed_ref, far_ref):
    unfold(got_ref[:, D:], far_ref)
    home, far = picks(slots_ref[...], scale_ref[...])
    home = jnp.concatenate(split(home), axis=1)
    far = jnp.concatenate(split(far), axis=1)
    turn = ((0,), (0,))
    for c in range(0, D, STEP):
        both = dot(home, got_ref[:, c:c + STEP], turn) + dot(far, far_ref[:, c:c + STEP], turn)
        mixed_ref[:, c:c + STEP] = (both[:TOK] + both[TOK:]).astype(BF)


def back_kernel(slots_ref, got_ref, grad_ref, far_ref):
    unfold(got_ref[:, D:], far_ref)
    home, far = picks(slots_ref[...])
    home, far = home.astype(BF), far.astype(BF)
    turn = ((0,), (0,))
    for c in range(0, D, STEP):
        grad_ref[:, c:c + STEP] = (
            dot(home, got_ref[:, c:c + STEP], turn) + dot(far, far_ref[:, c:c + STEP], turn)
        ).astype(BF)


def call(kernel, outs, *args, smem=0, scratch=(), flops=0):
    size = sum(a.size * a.dtype.itemsize for a in args)
    size += sum(o.size * o.dtype.itemsize for o in outs)
    vmem = pl.BlockSpec(memory_space=pltpu.VMEM)
    return pl.pallas_call(
        kernel,
        out_shape=outs,
        in_specs=[pl.BlockSpec(memory_space=pltpu.SMEM)] * smem + [vmem] * (len(args) - smem),
        out_specs=[vmem] * len(outs),
        scratch_shapes=list(scratch),
        compiler_params=pltpu.CompilerParams(vmem_limit_bytes=VMEM_LIMIT),
        cost_estimate=pl.CostEstimate(flops=flops, bytes_accessed=size, transcendentals=0),
    )(*args)


def shape(rows, cols, dtype=BF):
    return jax.ShapeDtypeStruct((rows, cols), dtype)


def exchange(values):
    return lax.all_to_all(values, "expert", split_axis=0, concat_axis=0, tiled=True)


def shards(tokens, cotangent, routes, route_weight, replica_pick, hot_experts, hot_holders,
           capacity, gate_weight, up_weight, down_weight):
    gate, up, down = gate_weight[0], up_weight[0], down_weight[0]
    rows = HOME + FAR
    product = 2 * rows * D * FF
    square = shape(TOK, TOK, F32)
    packed = shape(HOME, WIDE)
    far = shape(FAR, D)
    act, act32 = shape(rows, FF), shape(rows, FF, F32)
    far_scratch = pltpu.VMEM((FAR, D), BF)
    move = 2 * rows * TOK * D

    send_x, slots, scale = call(
        plan_kernel, [packed, square, square], hot_experts, hot_holders, capacity,
        routes, route_weight, replica_pick, tokens, smem=3, flops=move,
    )
    got_x = exchange(send_x)
    (send_g,) = call(grads_kernel, [packed], slots, scale, cotangent, flops=2 * move)
    got_g = exchange(send_g)
    send_out, far_x, hidden, gate_factor, up_factor = call(
        forward_kernel, [packed, far, act, act32, act32], got_x, gate, up, down,
        flops=3 * product,
    )
    got_out = exchange(send_out)
    send_back, far_g, back_gate, back_up = call(
        backward_kernel, [packed, far, act, act], got_g, gate, up, down, gate_factor, up_factor,
        flops=3 * product,
    )
    got_back = exchange(send_back)
    grad = shape(D, FF)
    (part_down,) = call(weight_kernel, [grad], got_g, far_g, hidden, flops=product)
    part_gate, part_up = call(
        weight_kernel, [grad, grad], got_x, far_x, back_gate, back_up, flops=2 * product
    )
    grads = [
        lax.psum_scatter(part, "dp", scatter_dimension=0, tiled=True)[None]
        for part in (part_gate, part_up, part_down)
    ]
    (mixed,) = call(
        mixed_kernel, [shape(TOK, D)], slots, scale, got_out, scratch=[far_scratch], flops=2 * move
    )
    (grad_tokens,) = call(
        back_kernel, [shape(TOK, D)], slots, got_back, scratch=[far_scratch], flops=move
    )
    return (mixed, grad_tokens, *grads)


def solution(mesh):
    tokens = P(("dp", "expert"), None)
    weights = P("expert", None, None)
    grads = P("expert", "dp", None)
    return jax.shard_map(
        shards,
        mesh=mesh,
        in_specs=(tokens,) * 5 + (P(),) * 3 + (weights,) * 3,
        out_specs=(tokens, tokens, grads, grads, grads),
        check_vma=False,
    )
```

profile of v0, /device:TPU:1, one launch (start us, length us, event | category | flops | bytes accessed | tf_op | source)
XLA Modules:
  0.0 246.6 jit_solution(8832576515933286471)
XLA Ops:
  7.2 1.4 copy.16.routes_ref
  8.6 1.4 copy.17.weight_ref
  10.0 1.4 copy.18.pick_ref
  11.4 5.3 %shard_map.146 = (bf16[512,2816]{1,0:T(8,128)(2,1)}, f32[128,128]{1,0:T(8,128)}, f32[128,128]{1,0:T(8,128)}) custom-call(s32[8]{0:T(128)} %hot_ref.1, s32[8]{0:T(128)} %holder_ref.1, s32[64]{0:T(128)} %cap_ref.1, s32[128,8]{1,0:T(8,128)} %copy.16.routes_ref, s32[128,8]{1,0:T(8,128)} %copy.17.weight_ref, s32[128,8]{1,0:T(8,128)} %copy.18.pick_ref, ...), custom_call_target="tpu_custom_call" | custom-call | flops 369098752 | bytes 3551552 | tf_op jit(solution)/shard_map/pallas_call | solution.py:231
  16.7 12.0 %all-to-all-start = ((bf16[64,8,2816]{2,1,0:T(8,128)(2,1)}), bf16[64,8,2816]{2,1,0:T(8,128)(2,1)S(1)}, u32[]{:S(2)}, u32[]{:S(2)}) async-start(bf16[64,8,2816]{2,1,0:T(8,128)(2,1)} %bitcast.21), calls=%async_computation | async-start | bytes 5767168 | tf_op jit(solution)/shard_map/all_to_all | solution.py:247
  28.7 4.3 %shard_map.149 = bf16[512,2816]{1,0:T(8,128)(2,1)} custom-call(f32[128,128]{1,0:T(8,128)} %get-tuple-element.19.slots_ref, f32[128,128]{1,0:T(8,128)} %get-tuple-element.20.scale_ref, bf16[128,2048]{1,0:T(8,128)(2,1)} %cot_ref.1), custom_call_target="tpu_custom_call" | custom-call | flops 738197504 | bytes 3538944 | tf_op jit(solution)/shard_map/pallas_call | solution.py:231
  32.9 32.1 %all-to-all-done = bf16[64,8,2816]{2,1,0:T(8,128)(2,1)S(1)} async-done(((bf16[64,8,2816]{2,1,0:T(8,128)(2,1)}), bf16[64,8,2816]{2,1,0:T(8,128)(2,1)S(1)}, u32[]{:S(2)}, u32[]{:S(2)}) %all-to-all-start) | async-done | bytes 2883616 | tf_op jit(solution)/shard_map/all_to_all | solution.py:247
  65.1 0.0 copy-start.1
  65.1 1.5 copy-done.1
  66.6 8.2 %all-to-all-start.2 = ((bf16[64,8,2816]{2,1,0:T(8,128)(2,1)}), bf16[64,8,2816]{2,1,0:T(8,128)(2,1)}, u32[]{:S(2)}, u32[]{:S(2)}) async-start(bf16[64,8,2816]{2,1,0:T(8,128)(2,1)} %bitcast.14), calls=%async_computation.2 | async-start | bytes 5767168 | tf_op jit(solution)/shard_map/all_to_all | solution.py:247
  74.8 0.2 reduce-scatter.8.cloned.1.call-start
  75.0 16.8 %shard_map.147 = (bf16[512,2816]{1,0:T(8,128)(2,1)}, bf16[192,2048]{1,0:T(8,128)(2,1)}, bf16[704,768]{1,0:T(8,128)(2,1)}, f32[704,768]{1,0:T(8,128)}, f32[704,768]{1,0:T(8,128)}) custom-call(bf16[512,2816]{1,0:T(8,128)(2,1)} %bitcast.18, bf16[2048,768]{1,0:T(8,128)(2,1)} %bitcast.22, bf16[2048,768]{1,0:T(8,128)(2,1)} %bitcast.24, bf16[2048,768]{1,0:T(8,128)(2,1)} %bitcast.26), custom_call_target="tpu_custom_call" | custom-call | flops 6643777536 | bytes 21397504 | tf_op jit(solution)/shard_map/pallas_call | solution.py:231
  91.8 18.7 %all-to-all-done.2 = bf16[64,8,2816]{2,1,0:T(8,128)(2,1)} async-done(((bf16[64,8,2816]{2,1,0:T(8,128)(2,1)}), bf16[64,8,2816]{2,1,0:T(8,128)(2,1)}, u32[]{:S(2)}, u32[]{:S(2)}) %all-to-all-start.2) | async-done | bytes 2883616 | tf_op jit(solution)/shard_map/all_to_all | solution.py:247
  110.5 18.3 %shard_map.150 = (bf16[512,2816]{1,0:T(8,128)(2,1)}, bf16[192,2048]{1,0:T(8,128)(2,1)}, bf16[704,768]{1,0:T(8,128)(2,1)}, bf16[704,768]{1,0:T(8,128)(2,1)}) custom-call(bf16[512,2816]{1,0:T(8,128)(2,1)} %bitcast.8.got_ref.home_ref, bf16[2048,768]{1,0:T(8,128)(2,1)} %bitcast.23, bf16[2048,768]{1,0:T(8,128)(2,1)} %bitcast.25, bf16[2048,768]{1,0:T(8,128)(2,1)} %bitcast.27, ...), custom_call_target="tpu_custom_call" | custom-call | flops 6643777536 | bytes 22478848 | tf_op jit(solution)/shard_map/pallas_call | solution.py:231
  128.8 8.2 %shard_map.153 = bf16[2048,768]{1,0:T(8,128)(2,1)} custom-call(bf16[512,2816]{1,0:T(8,128)(2,1)} %bitcast.8.got_ref.home_ref, bf16[192,2048]{1,0:T(8,128)(2,1)} %get-tuple-element.31.far_ref, bf16[704,768]{1,0:T(8,128)(2,1)} %get-tuple-element.32.refs_0_), custom_call_target="tpu_custom_call" | custom-call | flops 2214592512 | bytes 7897088 | tf_op jit(solution)/shard_map/pallas_call | solution.py:231
  137.0 0.0 reduce-scatter.8.cloned.1.call-update
  137.0 0.0 reduce-scatter.4.cloned.1.call-start
  137.0 11.9 %shard_map.152 = (bf16[2048,768]{1,0:T(8,128)(2,1)}, bf16[2048,768]{1,0:T(8,128)(2,1)}) custom-call(bf16[512,2816]{1,0:T(8,128)(2,1)} %bitcast.19, bf16[192,2048]{1,0:T(8,128)(2,1)} %get-tuple-element.26.far_ref, bf16[704,768]{1,0:T(8,128)(2,1)} %get-tuple-element.27.refs_0_, bf16[704,768]{1,0:T(8,128)(2,1)} %get-tuple-element.28.refs_1_), custom_call_target="tpu_custom_call" | custom-call | flops 4429185024 | bytes 12124160 | tf_op jit(solution)/shard_map/pallas_call | solution.py:231
  148.9 0.0 copy-start.2
  148.9 0.0 reduce-scatter.4.cloned.1.call-update
  148.9 0.0 reduce-scatter.6.cloned.1.call-start
  149.0 0.7 reduce-scatter.6.cloned.1.call-update
  149.7 1.3 copy-done.2
  150.9 43.1 %all_to_all.44 = bf16[64,8,2816]{2,1,0:T(8,128)(2,1)} all-to-all(bf16[64,8,2816]{2,1,0:T(8,128)(2,1)S(1)} %bitcast.20), channel_id=1, replica_groups=mesh['dp'=2,'expert'=64] {'expert'}, dimensions={0} | all-to-all | bytes 5767168 | tf_op jit(solution)/shard_map/all_to_all | solution.py:247
  194.0 5.7 %all-to-all-start.1 = ((bf16[64,8,2816]{2,1,0:T(8,128)(2,1)}), bf16[64,8,2816]{2,1,0:T(8,128)(2,1)S(1)}, u32[]{:S(2)}, u32[]{:S(2)}) async-start(bf16[64,8,2816]{2,1,0:T(8,128)(2,1)} %bitcast.17), calls=%async_computation.1 | async-start | bytes 5767168 | tf_op jit(solution)/shard_map/all_to_all | solution.py:247
  199.7 3.8 %shard_map.151 = bf16[128,2048]{1,0:T(8,128)(2,1)} custom-call(f32[128,128]{1,0:T(8,128)} %get-tuple-element.19.slots_ref, bf16[512,2816]{1,0:T(8,128)(2,1)} %bitcast.16), custom_call_target="tpu_custom_call" | custom-call | flops 369098752 | bytes 3473408 | tf_op jit(solution)/shard_map/pallas_call | solution.py:231
  203.5 30.5 %all-to-all-done.1 = bf16[64,8,2816]{2,1,0:T(8,128)(2,1)S(1)} async-done(((bf16[64,8,2816]{2,1,0:T(8,128)(2,1)}), bf16[64,8,2816]{2,1,0:T(8,128)(2,1)S(1)}, u32[]{:S(2)}, u32[]{:S(2)}) %all-to-all-start.1) | async-done | bytes 2883616 | tf_op jit(solution)/shard_map/all_to_all | solution.py:247
  234.1 0.0 copy-start
  234.1 1.5 copy-done
  235.6 4.5 %shard_map.148 = bf16[128,2048]{1,0:T(8,128)(2,1)} custom-call(f32[128,128]{1,0:T(8,128)} %get-tuple-element.19.slots_ref, f32[128,128]{1,0:T(8,128)} %get-tuple-element.20.scale_ref, bf16[512,2816]{1,0:T(8,128)(2,1)} %bitcast.15), custom_call_target="tpu_custom_call" | custom-call | flops 738197504 | bytes 3538944 | tf_op jit(solution)/shard_map/pallas_call | solution.py:231
  240.1 0.0 reduce-scatter.8.cloned.1.call-done
  240.1 0.0 reduce-scatter.4.cloned.1.call-done
  (1 shorter events, 0.0 us)
Async XLA Ops:
  16.7 48.4 %all-to-all-start = ((bf16[64,8,2816]{2,1,0:T(8,128)(2,1)}), bf16[64,8,2816]{2,1,0:T(8,128)(2,1)S(1)}, u32[]{:S(2)}, u32[]{:S(2)}) async-start(bf16[64,8,2816]{2,1,0:T(8,128)(2,1)} %bitcast.21), calls=%async_computation | async-start | bytes 5767168 | tf_op jit(solution)/shard_map/all_to_all | solution.py:247
  65.1 1.5 copy-start.1
  66.6 43.9 %all-to-all-start.2 = ((bf16[64,8,2816]{2,1,0:T(8,128)(2,1)}), bf16[64,8,2816]{2,1,0:T(8,128)(2,1)}, u32[]{:S(2)}, u32[]{:S(2)}) async-start(bf16[64,8,2816]{2,1,0:T(8,128)(2,1)} %bitcast.14), calls=%async_computation.2 | async-start | bytes 5767168 | tf_op jit(solution)/shard_map/all_to_all | solution.py:247
  74.8 165.3 %reduce-scatter.8.cloned.1.call-start = ((), (), s32[]{:S(2)}) async-start(), calls=%async_computation.9 | async-start | bytes 4718592 | tf_op jit(solution)/shard_map/reduce_scatter | solution.py:285
  137.0 103.1 %reduce-scatter.4.cloned.1.call-start = ((), (), s32[]{:S(2)}) async-start(), calls=%async_computation.7 | async-start | bytes 4718592 | tf_op jit(solution)/shard_map/reduce_scatter | solution.py:285
  148.9 2.0 copy-start.2
  148.9 91.1 %reduce-scatter.6.cloned.1.call-start = ((), (), s32[]{:S(2)}) async-start(), calls=%async_computation.8 | async-start | bytes 4718592 | tf_op jit(solution)/shard_map/reduce_scatter | solution.py:285
  194.0 40.0 %all-to-all-start.1 = ((bf16[64,8,2816]{2,1,0:T(8,128)(2,1)}), bf16[64,8,2816]{2,1,0:T(8,128)(2,1)S(1)}, u32[]{:S(2)}, u32[]{:S(2)}) async-start(bf16[64,8,2816]{2,1,0:T(8,128)(2,1)} %bitcast.17), calls=%async_computation.1 | async-start | bytes 5767168 | tf_op jit(solution)/shard_map/all_to_all | solution.py:247
  234.1 1.5 copy-start
Sparse Core Ops, SparseCore 0:
  137.1 14.1 reduce-scatter.7
  154.3 14.9 reduce-scatter.3
  172.2 14.9 reduce-scatter.5
where the time goes:
time: 251 us; the launch traced here: 247 us
  waiting for transfers between devices  82.1 us (33%)
  Pallas kernels  73 us (29%)
  blocking collectives  43.1 us (17%)
  starting transfers between devices  26.1 us (10%)
  between operations  13.8 us (5%)
  local copies, waits for them, and re-layouts  8.6 us (3%)
    all_to_all x3, waiting for transfers between devices, exchange(): lax.all_to_all(values, 'expert', split_axis=0, concat_axis=0, tiled=True)  81.4 us
    pallas_call x8, Pallas kernels, call(): pl.pallas_call(kernel, out_shape=outs, in_specs=[pl.BlockSpec(memory_spac...  73 us
    all_to_all x1, blocking collectives, exchange(): lax.all_to_all(values, 'expert', split_axis=0, concat_axis=0, tiled=True)  43.1 us
    all_to_all x3, starting transfers between devices, exchange(): lax.all_to_all(values, 'expert', split_axis=0, concat_axis=0, tiled=True)  25.8 us
    unnamed x9, local copies, waits for them, and re-layouts  8.6 us
  transfers between devices with their start and end apart: 6, of which 3 were waited for; matrix products, arithmetic and copies ran while one was open for 0% of the time, Pallas kernels for 17%

commit v1 on v0

--- a/solution.py
+++ b/solution.py
@@ -17,11 +17,12 @@
 FAR = EXPERTS * RCAP
 PARTS = 8
 PIECE = D // PARTS
+HALF = D // 2
 WIDE = D + RCAP * PIECE
 STEP = 256
 BF = jnp.bfloat16
 F32 = jnp.float32
-VMEM_LIMIT = 56 * 1024 * 1024
+VMEM_LIMIT = 32 * 1024 * 1024
 
 
 def dot(a, b, dims=((1,), (0,))):
@@ -77,39 +78,33 @@
 def plan_kernel(hot_ref, holder_ref, cap_ref, routes_ref, weight_ref, pick_ref, tokens_ref,
                 send_ref, slots_ref, scale_ref):
     lane = lax.broadcasted_iota(jnp.int32, (1, TOK), 1)
-    expert = lane % EXPERTS
-    far_lane = lane >= EXPERTS
     limit = jnp.zeros((1, TOK), jnp.int32)
     for e in range(EXPERTS):
         limit = jnp.where(lane == e, cap_ref[e], limit)
     hot = jnp.zeros((1, TOK), jnp.int32)
     for j in range(HOT):
-        here = expert == hot_ref[j]
-        hot = jnp.where(here, 1, hot)
+        hot = jnp.where(lane % EXPERTS == hot_ref[j], 1, hot)
         limit = jnp.where(
-            jnp.logical_and(here, far_lane), jnp.minimum(cap_ref[holder_ref[j]], RCAP), limit
+            lane == EXPERTS + hot_ref[j], jnp.minimum(cap_ref[holder_ref[j]], RCAP), limit
         )
-    far_value = jnp.where(far_lane, 1, 0)
-    present = jnp.zeros((TOK, TOK), F32)
-    scale = jnp.zeros((TOK, TOK), F32)
-    for k in range(TOPK):
-        replica = hot * pick_ref[:, k:k + 1]
-        match = jnp.logical_and(routes_ref[:, k:k + 1] == expert, replica == far_value)
-        present = jnp.where(match, 1.0, present)
-        scale = jnp.where(match, weight_ref[:, k:k + 1].astype(F32), scale)
     row = lax.broadcasted_iota(jnp.int32, (TOK, TOK), 0)
     col = lax.broadcasted_iota(jnp.int32, (TOK, TOK), 1)
-    before = (col < row).astype(F32).astype(BF)
-    same = (col == row).astype(F32).astype(BF)
-    rank = dot(before, present.astype(BF))
+    limit = jnp.sum(jnp.where(row == col, limit, 0), axis=1, keepdims=True)
+    hot = jnp.sum(jnp.where(row == col, hot, 0), axis=1, keepdims=True)
+    expert = row % EXPERTS
+    far_class = row // EXPERTS
+    present = jnp.zeros((TOK, TOK), F32)
+    scale = jnp.zeros((TOK, TOK), jnp.int32)
+    for k in range(TOPK):
+        replica = hot * pick_ref[k:k + 1, :]
+        match = jnp.logical_and(routes_ref[k:k + 1, :] == expert, replica == far_class)
+        present = jnp.where(match, 1.0, present)
+        scale = jnp.where(match, weight_ref[k:k + 1, :], scale)
+    rank = dot(present.astype(BF), (row < col).astype(F32).astype(BF))
     kept = jnp.logical_and(present > 0.0, rank < limit.astype(F32))
-    slots = jnp.where(kept, rank + 1.0, 0.0).astype(BF)
-    high = scale.astype(BF)
-    low = (scale - high.astype(F32)).astype(BF)
-    turn = ((0,), (0,))
-    slots = dot(slots, same, turn)
+    slots = jnp.where(kept, rank + 1.0, 0.0)
     slots_ref[...] = slots
-    scale_ref[...] = (dot(high, same, turn) + dot(low, same, turn)) * (1.0 / 4096.0)
+    scale_ref[...] = scale.astype(F32) * (1.0 / 4096.0)
     home, far = picks(slots)
     home, far = home.astype(BF), far.astype(BF)
     for c in range(0, D, STEP):
@@ -188,18 +183,22 @@
     outputs(send_ref, [(back_gate_ref, gate_ref), (back_up_ref, up_ref)])
 
 
-def weight_kernel(home_ref, far_ref, *refs):
-    count = len(refs) // 2
-
-    def step(n, carry):
-        cols = pl.ds(pl.multiple_of(n * STEP, STEP), STEP)
-        home, far = home_ref[:, cols], far_ref[:, cols]
-        for back, grad in zip(refs[:count], refs[count:]):
-            turn = ((0,), (0,))
-            grad[cols, :] = (dot(home, back[:HOME], turn) + dot(far, back[HOME:], turn)).astype(BF)
-        return carry
-
-    lax.fori_loop(0, D // STEP, step, 0)
+def weight_kernel(me_ref, home_ref, far_ref, *refs):
+    count = len(refs) // 3
+    backs, sends, keeps = refs[:count], refs[count:2 * count], refs[2 * count:]
+    turn = ((0,), (0,))
+    for first, grads in (((1 - me_ref[0]) * HALF, sends), (me_ref[0] * HALF, keeps)):
+
+        def step(n, carry, first=first, grads=grads):
+            rows = pl.ds(pl.multiple_of(n * STEP, STEP), STEP)
+            cols = pl.ds(pl.multiple_of(first + n * STEP, STEP), STEP)
+            home, far = home_ref[:, cols], far_ref[:, cols]
+            for back, grad in zip(backs, grads):
+                total = dot(home, back[:HOME], turn) + dot(far, back[HOME:], turn)
+                grad[rows, :] = total.astype(BF)
+            return carry
+
+        lax.fori_loop(0, HALF // STEP, step, 0)
 
 
 def mixed_kernel(slots_ref, scale_ref, got_ref, mixed_ref, far_ref):
@@ -261,7 +260,7 @@
 
     send_x, slots, scale = call(
         plan_kernel, [packed, square, square], hot_experts, hot_holders, capacity,
-        routes, route_weight, replica_pick, tokens, smem=3, flops=move,
+        routes.T, route_weight.T, replica_pick.T, tokens, smem=3, flops=move,
     )
     got_x = exchange(send_x)
     (send_g,) = call(grads_kernel, [packed], slots, scale, cotangent, flops=2 * move)
@@ -275,15 +274,19 @@
         backward_kernel, [packed, far, act, act], got_g, gate, up, down, gate_factor, up_factor,
         flops=3 * product,
     )
+    send_back, got_out = lax.optimization_barrier((send_back, got_out))
     got_back = exchange(send_back)
-    grad = shape(D, FF)
-    (part_down,) = call(weight_kernel, [grad], got_g, far_g, hidden, flops=product)
-    part_gate, part_up = call(
-        weight_kernel, [grad, grad], got_x, far_x, back_gate, back_up, flops=2 * product
+    half = shape(HALF, FF)
+    me = lax.axis_index("dp").reshape(1)
+    send_down, keep_down = call(
+        weight_kernel, [half] * 2, me, got_g, far_g, hidden, smem=1, flops=product
+    )
+    send_gate, send_up, keep_gate, keep_up = call(
+        weight_kernel, [half] * 4, me, got_x, far_x, back_gate, back_up, smem=1, flops=2 * product
     )
     grads = [
-        lax.psum_scatter(part, "dp", scatter_dimension=0, tiled=True)[None]
-        for part in (part_gate, part_up, part_down)
+        (keep.astype(F32) + lax.ppermute(send, "dp", ((0, 1), (1, 0))).astype(F32)).astype(BF)[None]
+        for send, keep in ((send_gate, keep_gate), (send_up, keep_up), (send_down, keep_down))
     ]
     (mixed,) = call(
         mixed_kernel, [shape(TOK, D)], slots, scale, got_out, scratch=[far_scratch], flops=2 * move

time: 251 us -> 194 us (0.77)
  the two profiles are of different devices: /device:TPU:1 before, /device:TPU:0 now
where the time goes in v1:
time: 194 us; the launch traced here: 193 us
  waiting for transfers between devices  72.3 us (37%)
  Pallas kernels  47.5 us (24%)
  local copies, waits for them, and re-layouts  34.2 us (18%)
  starting transfers between devices  32.8 us (17%)
  other arithmetic  4.81 us (2%)
    all_to_all x4, waiting for transfers between devices, exchange(): lax.all_to_all(values, 'expert', split_axis=0, concat_axis=0, tiled=True)  70.4 us
    pallas_call x8, Pallas kernels, call(): pl.pallas_call(kernel, out_shape=outs, in_specs=[pl.BlockSpec(memory_spac...  47.5 us
    unnamed x66, local copies, waits for them, and re-layouts  34.2 us
    all_to_all x4, starting transfers between devices, exchange(): lax.all_to_all(values, 'expert', split_axis=0, concat_axis=0, tiled=True)  32.1 us
    broadcast_in_dim x3, other arithmetic, shards(): (keep.astype(F32) + lax.ppermute(send, 'dp', ((0, 1), (1, 0))).astype(F32...  4.81 us
  transfers between devices with their start and end apart: 7, of which 6 were waited for; matrix products, arithmetic and copies ran while one was open for 3% of the time, Pallas kernels for 22%

profile of v1, /device:TPU:0, one launch (start us, length us, event | category | flops | bytes accessed | tf_op | source)
XLA Modules:
  0.0 192.5 jit_solution(9372169818887258379)
XLA Ops:
  5.7 2.1 %shard_map.146 = (bf16[512,2816]{1,0:T(8,128)(2,1)S(1)}, f32[128,128]{1,0:T(8,128)S(1)}, f32[128,128]{1,0:T(8,128)S(1)}) custom-call(s32[8]{0:T(128)S(1)} %copy-done.16, s32[8]{0:T(128)S(1)} %copy-done.17, s32[64]{0:T(128)S(1)} %copy-done.18, s32[8,128]{1,0:T(8,128)S(1)} %bitcast.33, s32[8,128]{1,0:T(8,128)S(1)} %bitcast.34, s32[8,128]{1,0:T(8,128)S(1)} %bitcast.35, ...), custom_call_target="tpu_custom_call" | custom-call | flops 369098752 | bytes 3551552 | tf_op jit(solution)/shard_map/pallas_call | solution.py:230
  7.8 1.5 copy-done.4
  9.4 11.6 %all-to-all-start.1 = ((bf16[64,8,2816]{2,1,0:T(8,128)(2,1)}), bf16[64,8,2816]{2,1,0:T(8,128)(2,1)S(1)}, u32[]{:S(2)}, u32[]{:S(2)}) async-start(bf16[64,8,2816]{2,1,0:T(8,128)(2,1)} %bitcast.26), calls=%async_computation.1 | async-start | bytes 5767168 | tf_op jit(solution)/shard_map/all_to_all | solution.py:246
  21.0 3.1 %shard_map.147 = bf16[512,2816]{1,0:T(8,128)(2,1)} custom-call(f32[128,128]{1,0:T(8,128)S(1)} %get-tuple-element.25.slots_ref, f32[128,128]{1,0:T(8,128)S(1)} %get-tuple-element.26.scale_ref, bf16[128,2048]{1,0:T(8,128)(2,1)S(1)} %copy-done.5), custom_call_target="tpu_custom_call" | custom-call | flops 738197504 | bytes 3538944 | tf_op jit(solution)/shard_map/pallas_call | solution.py:230
  24.1 35.1 %all-to-all-done.1 = bf16[64,8,2816]{2,1,0:T(8,128)(2,1)S(1)} async-done(((bf16[64,8,2816]{2,1,0:T(8,128)(2,1)}), bf16[64,8,2816]{2,1,0:T(8,128)(2,1)S(1)}, u32[]{:S(2)}, u32[]{:S(2)}) %all-to-all-start.1) | async-done | bytes 2883616 | tf_op jit(solution)/shard_map/all_to_all | solution.py:246
  59.3 6.8 %all-to-all-start = ((bf16[64,8,2816]{2,1,0:T(8,128)(2,1)}), bf16[64,8,2816]{2,1,0:T(8,128)(2,1)}, u32[]{:S(2)}, u32[]{:S(2)}) async-start(bf16[64,8,2816]{2,1,0:T(8,128)(2,1)} %bitcast.3), calls=%async_computation | async-start | bytes 5767168 | tf_op jit(solution)/shard_map/all_to_all | solution.py:246
  66.1 1.9 copy-done.6
  68.0 1.9 copy-done.8
  69.9 1.9 copy-done.10
  71.8 10.6 %shard_map.148 = (bf16[512,2816]{1,0:T(8,128)(2,1)S(1)}, bf16[192,2048]{1,0:T(8,128)(2,1)S(1)}, bf16[704,768]{1,0:T(8,128)(2,1)S(1)}, f32[704,768]{1,0:T(8,128)S(1)}, f32[704,768]{1,0:T(8,128)S(1)}) custom-call(bf16[512,2816]{1,0:T(8,128)(2,1)S(1)} %bitcast.22, bf16[2048,768]{1,0:T(8,128)(2,1)S(1)} %bitcast.27, bf16[2048,768]{1,0:T(8,128)(2,1)S(1)} %bitcast.29, ...), custom_call_target="tpu_custom_call" | custom-call | flops 6643777536 | bytes 21397504 | tf_op jit(solution)/shard_map/pallas_call | solution.py:230
  82.4 1.6 copy-done.3
  85.0 1.4 copy-done.23
  88.6 14.7 %all-to-all-done = bf16[64,8,2816]{2,1,0:T(8,128)(2,1)} async-done(((bf16[64,8,2816]{2,1,0:T(8,128)(2,1)}), bf16[64,8,2816]{2,1,0:T(8,128)(2,1)}, u32[]{:S(2)}, u32[]{:S(2)}) %all-to-all-start) | async-done | bytes 2883616 | tf_op jit(solution)/shard_map/all_to_all | solution.py:246
  103.3 7.2 %all-to-all-start.2 = ((bf16[64,8,2816]{2,1,0:T(8,128)(2,1)}), bf16[64,8,2816]{2,1,0:T(8,128)(2,1)S(1)}, u32[]{:S(2)}, u32[]{:S(2)}) async-start(bf16[64,8,2816]{2,1,0:T(8,128)(2,1)} %bitcast.25), calls=%async_computation.2 | async-start | bytes 5767168 | tf_op jit(solution)/shard_map/all_to_all | solution.py:246
  110.5 1.9 copy-done.7
  112.3 1.9 copy-done.9
  114.2 1.9 copy-done.11
  116.1 1.6 copy-done.24
  117.7 1.6 copy-done.26
  119.3 12.7 %shard_map.149 = (bf16[512,2816]{1,0:T(8,128)(2,1)S(1)}, bf16[192,2048]{1,0:T(8,128)(2,1)S(1)}, bf16[704,768]{1,0:T(8,128)(2,1)S(1)}, bf16[704,768]{1,0:T(8,128)(2,1)S(1)}) custom-call(bf16[512,2816]{1,0:T(8,128)(2,1)} %bitcast.4.got_ref.home_ref, bf16[2048,768]{1,0:T(8,128)(2,1)S(1)} %bitcast.28, bf16[2048,768]{1,0:T(8,128)(2,1)S(1)} %bitcast.30, ...), custom_call_target="tpu_custom_call" | custom-call | flops 6643777536 | bytes 22478848 | tf_op jit(solution)/shard_map/pallas_call | solution.py:230
  132.1 1.5 copy-done.2
  136.5 10.4 %all-to-all-done.2 = bf16[64,8,2816]{2,1,0:T(8,128)(2,1)S(1)} async-done(((bf16[64,8,2816]{2,1,0:T(8,128)(2,1)}), bf16[64,8,2816]{2,1,0:T(8,128)(2,1)S(1)}, u32[]{:S(2)}, u32[]{:S(2)}) %all-to-all-start.2) | async-done | bytes 2883616 | tf_op jit(solution)/shard_map/all_to_all | solution.py:246
  146.9 6.5 %all-to-all-start.3 = ((bf16[64,8,2816]{2,1,0:T(8,128)(2,1)}), bf16[64,8,2816]{2,1,0:T(8,128)(2,1)}, u32[]{:S(2)}, u32[]{:S(2)}) async-start(bf16[64,8,2816]{2,1,0:T(8,128)(2,1)} %bitcast.24), calls=%async_computation.3 | async-start | bytes 5767168 | tf_op jit(solution)/shard_map/all_to_all | solution.py:246
  155.8 6.2 %shard_map.153 = (bf16[1024,768]{1,0:T(8,128)(2,1)S(1)}, bf16[1024,768]{1,0:T(8,128)(2,1)S(1)}) custom-call(s32[1]{0:T(128)} %bitcast.14.me_ref, bf16[512,2816]{1,0:T(8,128)(2,1)} %bitcast.4.got_ref.home_ref, bf16[192,2048]{1,0:T(8,128)(2,1)S(1)} %copy-done.22, bf16[704,768]{1,0:T(8,128)(2,1)S(1)} %copy-done.20), custom_call_target="tpu_custom_call" | custom-call | flops 2214592512 | bytes 7897092 | tf_op jit(solution)/shard_map/pallas_call | solution.py:230
  162.1 6.4 %shard_map.152 = (bf16[1024,768]{1,0:T(8,128)(2,1)S(1)}, bf16[1024,768]{1,0:T(8,128)(2,1)S(1)}, bf16[1024,768]{1,0:T(8,128)(2,1)S(1)}, bf16[1024,768]{1,0:T(8,128)(2,1)S(1)}) custom-call(s32[1]{0:T(128)} %bitcast.14.me_ref, bf16[512,2816]{1,0:T(8,128)(2,1)S(1)} %bitcast.23, bf16[192,2048]{1,0:T(8,128)(2,1)S(1)} %copy-done.32, ...), custom_call_target="tpu_custom_call" | custom-call | flops 4429185024 | bytes 12124164 | tf_op jit(solution)/shard_map/pallas_call | solution.py:230
  169.2 1.6 fusion.2
  170.8 1.3 collective-permute-done.1
  172.1 1.6 fusion.1
  174.4 1.6 fusion
  176.0 2.6 %shard_map.150 = bf16[128,2048]{1,0:T(8,128)(2,1)} custom-call(f32[128,128]{1,0:T(8,128)S(1)} %get-tuple-element.25.slots_ref, f32[128,128]{1,0:T(8,128)S(1)} %get-tuple-element.26.scale_ref, bf16[512,2816]{1,0:T(8,128)(2,1)S(1)} %bitcast.21), custom_call_target="tpu_custom_call" | custom-call | flops 738197504 | bytes 3538944 | tf_op jit(solution)/shard_map/pallas_call | solution.py:230
  178.6 10.2 %all-to-all-done.3 = bf16[64,8,2816]{2,1,0:T(8,128)(2,1)} async-done(((bf16[64,8,2816]{2,1,0:T(8,128)(2,1)}), bf16[64,8,2816]{2,1,0:T(8,128)(2,1)}, u32[]{:S(2)}, u32[]{:S(2)}) %all-to-all-start.3) | async-done | bytes 2883616 | tf_op jit(solution)/shard_map/all_to_all | solution.py:246
  188.7 3.8 %shard_map.151 = bf16[128,2048]{1,0:T(8,128)(2,1)} custom-call(f32[128,128]{1,0:T(8,128)S(1)} %get-tuple-element.25.slots_ref, bf16[512,2816]{1,0:T(8,128)(2,1)} %bitcast.13.got_ref), custom_call_target="tpu_custom_call" | custom-call | flops 369098752 | bytes 3473408 | tf_op jit(solution)/shard_map/pallas_call | solution.py:230
  (59 shorter events, 14.9 us)
Async XLA Ops:
  0.6 1.0 copy-start.12
  7.8 1.6 copy-start.4
  9.4 11.6 %copy-start.5 = (bf16[128,2048]{1,0:T(8,128)(2,1)S(1)}, bf16[128,2048]{1,0:T(8,128)(2,1)}, u32[]{:S(2)}) copy-start(bf16[128,2048]{1,0:T(8,128)(2,1)} %cot_ref.1) | copy-start | bytes 1572868
  9.4 49.9 %all-to-all-start.1 = ((bf16[64,8,2816]{2,1,0:T(8,128)(2,1)}), bf16[64,8,2816]{2,1,0:T(8,128)(2,1)S(1)}, u32[]{:S(2)}, u32[]{:S(2)}) async-start(bf16[64,8,2816]{2,1,0:T(8,128)(2,1)} %bitcast.26), calls=%async_computation.1 | async-start | bytes 5767168 | tf_op jit(solution)/shard_map/all_to_all | solution.py:246
  59.3 6.8 %copy-start = (bf16[64,8,2816]{2,1,0:T(8,128)(2,1)}, bf16[64,8,2816]{2,1,0:T(8,128)(2,1)S(1)}, u32[]{:S(2)}) copy-start(bf16[64,8,2816]{2,1,0:T(8,128)(2,1)S(1)} %all-to-all-done.1) | copy-start | bytes 8650756
  59.3 44.0 %all-to-all-start = ((bf16[64,8,2816]{2,1,0:T(8,128)(2,1)}), bf16[64,8,2816]{2,1,0:T(8,128)(2,1)}, u32[]{:S(2)}, u32[]{:S(2)}) async-start(bf16[64,8,2816]{2,1,0:T(8,128)(2,1)} %bitcast.3), calls=%async_computation | async-start | bytes 5767168 | tf_op jit(solution)/shard_map/all_to_all | solution.py:246
  66.1 1.9 copy-start.6
  68.0 1.9 copy-start.8
  69.9 1.9 copy-start.10
  82.4 1.6 copy-start.3
  84.0 1.0 copy-start.19
  85.0 1.4 copy-start.23
  86.4 1.3 copy-start.25
  103.3 43.6 %all-to-all-start.2 = ((bf16[64,8,2816]{2,1,0:T(8,128)(2,1)}), bf16[64,8,2816]{2,1,0:T(8,128)(2,1)S(1)}, u32[]{:S(2)}, u32[]{:S(2)}) async-start(bf16[64,8,2816]{2,1,0:T(8,128)(2,1)} %bitcast.25), calls=%async_computation.2 | async-start | bytes 5767168 | tf_op jit(solution)/shard_map/all_to_all | solution.py:246
  110.5 1.9 copy-start.7
  112.3 1.9 copy-start.9
  114.2 1.9 copy-start.11
  116.1 1.6 copy-start.24
  117.7 1.6 copy-start.26
  132.1 1.5 copy-start.2
  134.5 1.0 copy-start.27
  135.5 1.0 copy-start.29
  146.9 41.9 %all-to-all-start.3 = ((bf16[64,8,2816]{2,1,0:T(8,128)(2,1)}), bf16[64,8,2816]{2,1,0:T(8,128)(2,1)}, u32[]{:S(2)}, u32[]{:S(2)}) async-start(bf16[64,8,2816]{2,1,0:T(8,128)(2,1)} %bitcast.24), calls=%async_computation.3 | async-start | bytes 5767168 | tf_op jit(solution)/shard_map/all_to_all | solution.py:246
  153.4 1.2 copy-start.20
  154.7 1.1 copy-start.22
  155.8 6.3 %copy-start.1 = (bf16[64,8,2816]{2,1,0:T(8,128)(2,1)S(1)}, bf16[64,8,2816]{2,1,0:T(8,128)(2,1)}, u32[]{:S(2)}) copy-start(bf16[64,8,2816]{2,1,0:T(8,128)(2,1)} %copy-done) | copy-start | bytes 8650756
  155.8 6.3 %copy-start.28 = (bf16[704,768]{1,0:T(8,128)(2,1)S(1)}, bf16[704,768]{1,0:T(8,128)(2,1)}, u32[]{:S(2)}) copy-start(bf16[704,768]{1,0:T(8,128)(2,1)} %copy-done.27) | copy-start | bytes 3244036
  155.8 6.3 %copy-start.30 = (bf16[704,768]{1,0:T(8,128)(2,1)S(1)}, bf16[704,768]{1,0:T(8,128)(2,1)}, u32[]{:S(2)}) copy-start(bf16[704,768]{1,0:T(8,128)(2,1)} %copy-done.29) | copy-start | bytes 3244036
  155.8 6.3 %copy-start.32 = (bf16[192,2048]{1,0:T(8,128)(2,1)S(1)}, bf16[192,2048]{1,0:T(8,128)(2,1)}, u32[]{:S(2)}) copy-start(bf16[192,2048]{1,0:T(8,128)(2,1)} %copy-done.31) | copy-start | bytes 2359300
  162.0 7.2 %collective-permute-start.2 = (bf16[1024,768]{1,0:T(8,128)(2,1)S(1)}, bf16[1024,768]{1,0:T(8,128)(2,1)S(1)}, u32[]{:S(2)}, u32[]{:S(2)}) collective-permute-start(bf16[1024,768]{1,0:T(8,128)(2,1)S(1)} %get-tuple-element.44), channel_id=1, source_target_pairs={{0,64},{64,0},{1,65},{65,1},{2,66},{66,2},{3,67},{67,3},{4,68},{68... | collective-permute-start | bytes 4718600 | tf_op jit(solution)/shard_map/ppermute | solution.py:288
  168.5 3.6 %collective-permute-start.1 = (bf16[1024,768]{1,0:T(8,128)(2,1)S(1)}, bf16[1024,768]{1,0:T(8,128)(2,1)S(1)}, u32[]{:S(2)}, u32[]{:S(2)}) collective-permute-start(bf16[1024,768]{1,0:T(8,128)(2,1)S(1)} %get-tuple-element.40), channel_id=1, source_target_pairs={{0,64},{64,0},{1,65},{65,1},{2,66},{66,2},{3,67},{67,3},{4,68},{68... | collective-permute-start | bytes 4718600 | tf_op jit(solution)/shard_map/ppermute | solution.py:288
  169.1 5.3 %collective-permute-start = (bf16[1024,768]{1,0:T(8,128)(2,1)S(1)}, bf16[1024,768]{1,0:T(8,128)(2,1)S(1)}, u32[]{:S(2)}, u32[]{:S(2)}) collective-permute-start(bf16[1024,768]{1,0:T(8,128)(2,1)S(1)} %get-tuple-element.38), channel_id=1, source_target_pairs={{0,64},{64,0},{1,65},{65,1},{2,66},{66,2},{3,67},{67,3},{4,68},{68... | collective-permute-start | bytes 4718600 | tf_op jit(solution)/shard_map/ppermute | solution.py:288
  (8 other events, 5.8 us)

commit v2 on v1

v2 whole, which is shorter than its diff:
```python
import jax
import jax.numpy as jnp
from jax import lax
from jax.experimental import pallas as pl
from jax.experimental.pallas import tpu as pltpu
from jax.sharding import PartitionSpec as P

D = 2048
FF = 768
TOPK = 8
HOT = 8
CAP = 8
RCAP = 3
TOK = 128
EXPERTS = 64
HOME = EXPERTS * CAP
FAR = EXPERTS * RCAP
PARTS = 8
PIECE = D // PARTS
FOLD = RCAP * PIECE
WIDE = D + FOLD
ROWS = HOME + FAR
GROUP = 32
HALF = D // 2
STEP = 256
BF = jnp.bfloat16
F32 = jnp.float32
TURN = ((0,), (0,))
MIB = 1024 * 1024


def dot(a, b, dims=((1,), (0,))):
    return lax.dot_general(a, b, (dims, ((), ())), preferred_element_type=F32)


def fold_matrix(transposed=False):
    size = GROUP * PARTS
    row = lax.broadcasted_iota(jnp.int32, (size, size), 0)
    col = lax.broadcasted_iota(jnp.int32, (size, size), 1)
    if transposed:
        row, col = col, row
    return (col == (row % GROUP) * PARTS + row // GROUP).astype(F32).astype(BF)


def unfold(folded, rows_ref):
    order = fold_matrix()
    for first in range(0, EXPERTS, GROUP):
        flat = dot(order, folded[first * PARTS:(first + GROUP) * PARTS, :]).astype(BF)
        for i in range(PARTS):
            for f in range(RCAP):
                at = f * EXPERTS + first
                rows_ref[at:at + GROUP, i * PIECE:(i + 1) * PIECE] = flat[
                    i * GROUP:(i + 1) * GROUP, f * PIECE:(f + 1) * PIECE
                ]


def fold(rows, folded_ref):
    order = fold_matrix(transposed=True)
    for first in range(0, EXPERTS, GROUP):
        flat = jnp.concatenate(
            [
                jnp.concatenate(
                    [
                        rows[f * EXPERTS + first:f * EXPERTS + first + GROUP,
                             i * PIECE:(i + 1) * PIECE]
                        for f in range(RCAP)
                    ],
                    axis=1,
                )
                for i in range(PARTS)
            ],
            axis=0,
        )
        folded_ref[first * PARTS:(first + GROUP) * PARTS, :] = dot(order, flat).astype(BF)


def home_picks(slots, scale=None):
    s = lax.broadcasted_iota(jnp.int32, (EXPERTS, CAP, TOK), 1).astype(F32) + 1.0
    value = F32(1.0) if scale is None else scale[:EXPERTS][:, None, :]
    return jnp.where(slots[:EXPERTS][:, None, :] == s, value, 0.0).reshape(HOME, TOK)


def far_picks(slots, scale=None):
    value = F32(1.0) if scale is None else scale[EXPERTS:]
    return jnp.concatenate(
        [jnp.where(slots[EXPERTS:] == F32(f + 1), value, 0.0) for f in range(RCAP)], axis=0
    )


def split(values):
    high = values.astype(BF)
    return high, (values - high.astype(F32)).astype(BF)


def plan_kernel(hot_hbm, holder_hbm, cap_hbm, routes_hbm, weight_hbm, pick_hbm, tokens_hbm,
                send_hbm, slots_ref, scale_ref, hot_ref, holder_ref, cap_ref, routes_ref,
                weight_ref, pick_ref, tokens_ref, send_ref, sems, out_sems):
    copies = [
        pltpu.make_async_copy(src, dst, sems.at[i])
        for i, (src, dst) in enumerate(
            (
                (hot_hbm, hot_ref), (holder_hbm, holder_ref), (cap_hbm, cap_ref),
                (routes_hbm, routes_ref), (pick_hbm, pick_ref), (weight_hbm, weight_ref),
                (tokens_hbm, tokens_ref),
            )
        )
    ]
    for copy in copies:
        copy.start()
    for copy in copies[:-1]:
        copy.wait()
    lane = lax.broadcasted_iota(jnp.int32, (1, TOK), 1)
    limit = jnp.zeros((1, TOK), jnp.int32)
    for e in range(EXPERTS):
        limit = jnp.where(lane == e, cap_ref[e], limit)
    hot = jnp.zeros((1, TOK), jnp.int32)
    for j in range(HOT):
        hot = jnp.where(lane % EXPERTS == hot_ref[j], 1, hot)
        limit = jnp.where(
            lane == EXPERTS + hot_ref[j], jnp.minimum(cap_ref[holder_ref[j]], RCAP), limit
        )
    row = lax.broadcasted_iota(jnp.int32, (TOK, TOK), 0)
    col = lax.broadcasted_iota(jnp.int32, (TOK, TOK), 1)
    limit = jnp.sum(jnp.where(row == col, limit, 0), axis=1, keepdims=True)
    hot = jnp.sum(jnp.where(row == col, hot, 0), axis=1, keepdims=True)
    expert = row % EXPERTS
    far_class = row // EXPERTS
    present = jnp.zeros((TOK, TOK), F32)
    scale = jnp.zeros((TOK, TOK), jnp.int32)
    for k in range(TOPK):
        replica = hot * pick_ref[k:k + 1, :]
        match = jnp.logical_and(routes_ref[k:k + 1, :] == expert, replica == far_class)
        present = jnp.where(match, 1.0, present)
        scale = jnp.where(match, weight_ref[k:k + 1, :], scale)
    rank = dot(present.astype(BF), (row < col).astype(F32).astype(BF))
    kept = jnp.logical_and(present > 0.0, rank < limit.astype(F32))
    slots = jnp.where(kept, rank + 1.0, 0.0)
    slots_ref[...] = slots
    scale_ref[...] = scale.astype(F32) * (1.0 / 4096.0)
    home = home_picks(slots).astype(BF)
    copies[-1].wait()
    sends = []
    for n in range(4):
        cols = slice(n * 2 * STEP, (n + 1) * 2 * STEP)
        send_ref[:, cols] = dot(home, tokens_ref[:, cols]).astype(BF)
        sends.append(
            pltpu.make_async_copy(send_ref.at[:, cols], send_hbm.at[:, cols], out_sems.at[n])
        )
        sends[-1].start()
    fold(dot(far_picks(slots).astype(BF), tokens_ref[...]).astype(BF), send_ref.at[:, D:])
    sends.append(
        pltpu.make_async_copy(send_ref.at[:, D:], send_hbm.at[:, D:], out_sems.at[len(sends)])
    )
    sends[-1].start()
    for copy in sends:
        copy.wait()


def grads_kernel(slots_ref, scale_ref, cot_ref, send_ref, both_ref):
    slots, scale = slots_ref[...], scale_ref[...]
    both_ref[:TOK, :] = cot_ref[...]
    both_ref[TOK:, :] = cot_ref[...]
    home = jnp.concatenate(split(home_picks(slots, scale)), axis=1)
    for c in range(0, D, 2 * STEP):
        cols = slice(c, c + 2 * STEP)
        send_ref[:, cols] = dot(home, both_ref[:, cols]).astype(BF)
    far = jnp.concatenate(split(far_picks(slots, scale)), axis=1)
    fold(dot(far, both_ref[...]).astype(BF), send_ref.at[:, D:])


ACROSS = ((1,), (1,))
BLOCKS = ((HOME, FAR), (0, HOME // 2), (HOME // 2, HOME // 2))


def forward_kernel(got_ref, gate_ref, up_ref, down_ref, send_ref, far_ref, hidden_ref,
                   gate_factor_ref, up_factor_ref):
    unfold(got_ref[:, D:], far_ref)
    for first, count in BLOCKS:
        here = slice(first, first + count)
        x = far_ref[...] if first == HOME else got_ref[here, :D]
        pre_gate = dot(x, gate_ref[...])
        pre_up = dot(x, up_ref[...])
        sigma = jax.nn.sigmoid(pre_gate)
        active = pre_gate * sigma
        gate_factor_ref[here, :] = pre_up * sigma * (1.0 + pre_gate * (1.0 - sigma))
        up_factor_ref[here, :] = active
        hidden = (active * pre_up).astype(BF)
        hidden_ref[here, :] = hidden
        out = dot(hidden, down_ref[...], ACROSS).astype(BF)
        if first == HOME:
            fold(out, send_ref.at[:, D:])
        else:
            send_ref[here, :D] = out


def backward_kernel(got_ref, gate_ref, up_ref, down_ref, gate_factor_ref, up_factor_ref, send_ref,
                    far_ref, back_gate_ref, back_up_ref):
    unfold(got_ref[:, D:], far_ref)
    for first, count in BLOCKS:
        here = slice(first, first + count)
        g = far_ref[...] if first == HOME else got_ref[here, :D]
        back_hidden = dot(g, down_ref[...])
        back_gate = (back_hidden * gate_factor_ref[here, :]).astype(BF)
        back_up = (back_hidden * up_factor_ref[here, :]).astype(BF)
        back_gate_ref[here, :] = back_gate
        back_up_ref[here, :] = back_up
        back = dot(back_gate, gate_ref[...], ACROSS) + dot(back_up, up_ref[...], ACROSS)
        if first == HOME:
            fold(back.astype(BF), send_ref.at[:, D:])
        else:
            send_ref[here, :D] = back.astype(BF)


def weight_kernel(me_ref, home_ref, far_ref, *refs):
    count = len(refs) // 3
    backs, sends, keeps = refs[:count], refs[count:2 * count], refs[2 * count:]
    for half, grads in ((1 - me_ref[0], sends), (me_ref[0], keeps)):

        def step(n, carry, half=half, grads=grads):
            rows = pl.ds(pl.multiple_of(n * STEP, STEP), STEP)
            cols = pl.ds(pl.multiple_of(half * HALF + n * STEP, STEP), STEP)
            home, far = home_ref[:, cols], far_ref[:, cols]
            for back, grad in zip(backs, grads):
                total = dot(home, back[:HOME, :], TURN) + dot(far, back[HOME:, :], TURN)
                grad[rows, :] = total.astype(BF)
            return carry

        lax.fori_loop(0, HALF // STEP, step, 0)


def mixed_kernel(slots_ref, scale_ref, got_ref, mixed_ref, home_ones_ref, far_ones_ref, far_ref):
    unfold(got_ref[:, D:], far_ref)
    slots, scale = slots_ref[...], scale_ref[...]
    home = jnp.concatenate(split(home_picks(slots, scale)), axis=1)
    far = jnp.concatenate(split(far_picks(slots, scale)), axis=1)
    for c in range(0, D, STEP):
        cols = slice(c, c + STEP)
        both = dot(home, got_ref[:, cols], TURN) + dot(far, far_ref[:, cols], TURN)
        mixed_ref[:, cols] = (both[:TOK] + both[TOK:]).astype(BF)
    home_ones_ref[...] = home_picks(slots).T.astype(BF)
    far_ones_ref[...] = far_picks(slots).T.astype(BF)


def back_kernel(home_ref, far_ones_ref, got_ref, grad_ref, far_ref):
    unfold(got_ref[:, D:], far_ref)
    for c in range(0, D, 2 * STEP):
        cols = slice(c, c + 2 * STEP)
        grad_ref[:, cols] = (
            dot(home_ref[...], got_ref[:, cols]) + dot(far_ones_ref[...], far_ref[:, cols])
        ).astype(BF)


VMEM = pl.BlockSpec(memory_space=pltpu.VMEM)
SMEM = pl.BlockSpec(memory_space=pltpu.SMEM)
HBM = pl.BlockSpec(memory_space=pltpu.HBM)


def call(kernel, outs, args, flops, scratch=(), limit=32, in_specs=None, out_specs=None):
    size = sum(a.size * a.dtype.itemsize for a in args)
    size += sum(o.size * o.dtype.itemsize for o in outs)
    return pl.pallas_call(
        kernel,
        out_shape=outs,
        in_specs=in_specs or [VMEM] * len(args),
        out_specs=out_specs or [VMEM] * len(outs),
        scratch_shapes=list(scratch),
        compiler_params=pltpu.CompilerParams(vmem_limit_bytes=limit * MIB),
        cost_estimate=pl.CostEstimate(flops=flops, bytes_accessed=size, transcendentals=0),
    )(*args)


def shape(rows, cols, dtype=BF):
    return jax.ShapeDtypeStruct((rows, cols), dtype)


def exchange(values):
    return lax.all_to_all(values, "expert", split_axis=0, concat_axis=0, tiled=True)


def shards(tokens, cotangent, routes, route_weight, replica_pick, hot_experts, hot_holders,
           capacity, gate_weight, up_weight, down_weight):
    gate, up, down = gate_weight[0], up_weight[0], down_weight[0]
    product = 2 * ROWS * D * FF
    move = 2 * ROWS * TOK * D
    square = shape(TOK, TOK, F32)
    packed, far = shape(HOME, WIDE), shape(FAR, D)
    act, act32 = shape(ROWS, FF), shape(ROWS, FF, F32)
    far_scratch = pltpu.VMEM((FAR, D), BF)
    dma = pltpu.SemaphoreType.DMA

    send_x, slots, scale = call(
        plan_kernel,
        [packed, square, square],
        (hot_experts, hot_holders, capacity, routes.T, route_weight.T, replica_pick.T, tokens),
        move,
        [pltpu.SMEM((HOT,), jnp.int32), pltpu.SMEM((HOT,), jnp.int32),
         pltpu.SMEM((EXPERTS,), jnp.int32)]
        + [pltpu.VMEM((TOPK, TOK), jnp.int32)] * 3
        + [pltpu.VMEM((TOK, D), BF), pltpu.VMEM((HOME, WIDE), BF), dma((7,)), dma((5,))],
        60,
        [HBM] * 7,
        [HBM, VMEM, VMEM],
    )
    got_x = exchange(send_x)
    (send_g,) = call(
        grads_kernel, [packed], (slots, scale, cotangent), 2 * move,
        [pltpu.VMEM((2 * TOK, D), BF)],
    )
    got_g = exchange(send_g)
    send_out, far_x, hidden, gate_factor, up_factor = call(
        forward_kernel, [packed, far, act, act32, act32], (got_x, gate, up, down), 3 * product
    )
    got_out = exchange(send_out)
    send_back, far_g, back_gate, back_up = call(
        backward_kernel, [packed, far, act, act],
        (got_g, gate, up, down, gate_factor, up_factor), 3 * product,
    )
    send_back, got_out = lax.optimization_barrier((send_back, got_out))
    got_back = exchange(send_back)
    half = shape(HALF, FF)
    me = lax.axis_index("dp").reshape(1)
    send_down, keep_down = call(
        weight_kernel, [half] * 2, (me, got_g, far_g, hidden), product,
        in_specs=[SMEM] + [VMEM] * 3,
    )
    send_gate, send_up, keep_gate, keep_up = call(
        weight_kernel, [half] * 4, (me, got_x, far_x, back_gate, back_up), 2 * product,
        in_specs=[SMEM] + [VMEM] * 4,
    )
    grads = [
        (keep.astype(F32) + lax.ppermute(sent, "dp", ((0, 1), (1, 0))).astype(F32)).astype(BF)[None]
        for sent, keep in ((send_gate, keep_gate), (send_up, keep_up), (send_down, keep_down))
    ]
    mixed, home_ones, far_ones = call(
        mixed_kernel, [shape(TOK, D), shape(TOK, HOME), shape(TOK, FAR)], (slots, scale, got_out),
        2 * move, [far_scratch],
    )
    (grad_tokens,) = call(
        back_kernel, [shape(TOK, D)], (home_ones, far_ones, got_back), move, [far_scratch]
    )
    return (mixed, grad_tokens, *grads)


def solution(mesh):
    tokens = P(("dp", "expert"), None)
    weights = P("expert", None, None)
    grads = P("expert", "dp", None)
    return jax.shard_map(
        shards,
        mesh=mesh,
        in_specs=(tokens,) * 5 + (P(),) * 3 + (weights,) * 3,
        out_specs=(tokens, tokens, grads, grads, grads),
        check_vma=False,
    )
```

time: 194 us -> 189 us (0.974)
  local copies, waits for them, and re-layouts: 34.2 us -> 27.5 us
  waiting for transfers between devices: 72.3 us -> 77.3 us
  Pallas kernels: 47.5 us -> 44.5 us
    unnamed x66 -> x54, local copies, waits for them, and re-layouts: 34.2 us -> 27.5 us
    all_to_all x4, waiting for transfers between devices: 70.4 us -> 75.5 us  [exchange(): lax.all_to_all(values, 'expert', split_axis=0, concat_axis=0, tiled=True)]
    pallas_call x8, Pallas kernels: 47.5 us -> 44.5 us  [call(): pl.pallas_call(kernel, out_shape=outs, in_specs=in_specs or [VMEM] * len(...]
  transfers between devices with their start and end apart: 7 -> 7, of which waited for: 6 -> 6; matrix products, arithmetic and copies ran while one was open for 3% -> 2% of each run, Pallas kernels for 22% -> 20%
where the time goes in v2:
time: 189 us; the launch traced here: 188 us
  waiting for transfers between devices  77.3 us (41%)
  Pallas kernels  44.5 us (24%)
  starting transfers between devices  32.9 us (17%)
  local copies, waits for them, and re-layouts  27.5 us (15%)
  other arithmetic  4.63 us (2%)
    all_to_all x4, waiting for transfers between devices, exchange(): lax.all_to_all(values, 'expert', split_axis=0, concat_axis=0, tiled=True)  75.5 us
    pallas_call x8, Pallas kernels, call(): pl.pallas_call(kernel, out_shape=outs, in_specs=in_specs or [VMEM] * len(...  44.5 us
    all_to_all x4, starting transfers between devices, exchange(): lax.all_to_all(values, 'expert', split_axis=0, concat_axis=0, tiled=True)  31.9 us
    unnamed x54, local copies, waits for them, and re-layouts  27.5 us
    broadcast_in_dim x3, other arithmetic, shards(): (keep.astype(F32) + lax.ppermute(sent, 'dp', ((0, 1), (1, 0))).astype(F32...  4.63 us
  transfers between devices with their start and end apart: 7, of which 6 were waited for; matrix products, arithmetic and copies ran while one was open for 2% of the time, Pallas kernels for 20%

profile of v2, /device:TPU:0, one launch (start us, length us, event | category | flops | bytes accessed | tf_op | source)
XLA Modules:
  0.0 187.7 jit_solution(4510078626788660650)
XLA Ops:
  0.6 3.9 %shard_map.146 = (bf16[512,2816]{1,0:T(8,128)(2,1)}, f32[128,128]{1,0:T(8,128)}, f32[128,128]{1,0:T(8,128)}) custom-call(s32[8]{0:T(128)} %hot_hbm.1, s32[8]{0:T(128)} %holder_hbm.1, s32[64]{0:T(128)} %cap_hbm.1, s32[8,128]{1,0:T(8,128)} %bitcast.33, s32[8,128]{1,0:T(8,128)} %bitcast.34, s32[8,128]{1,0:T(8,128)} %bitcast.35, bf16[128,2048]{1,0:T(8,128)(2,1)} %tokens_hbm.1), custom_call_target="tpu_custom_call" | custom-call | flops 369098752 | bytes 3551552 | tf_op jit(solution)/shard_map/pallas_call | solution.py:261
  4.6 11.6 %all-to-all-start.1 = ((bf16[64,8,2816]{2,1,0:T(8,128)(2,1)}), bf16[64,8,2816]{2,1,0:T(8,128)(2,1)S(1)}, u32[]{:S(2)}, u32[]{:S(2)}) async-start(bf16[64,8,2816]{2,1,0:T(8,128)(2,1)} %bitcast.32), calls=%async_computation.1 | async-start | bytes 5767168 | tf_op jit(solution)/shard_map/all_to_all | solution.py:277
  16.3 2.8 %shard_map.147 = bf16[512,2816]{1,0:T(8,128)(2,1)} custom-call(f32[128,128]{1,0:T(8,128)S(1)} %copy-done.5, f32[128,128]{1,0:T(8,128)S(1)} %copy-done.6, bf16[128,2048]{1,0:T(8,128)(2,1)S(1)} %copy-done.4), custom_call_target="tpu_custom_call" | custom-call | flops 738197504 | bytes 3538944 | tf_op jit(solution)/shard_map/pallas_call | solution.py:261
  19.1 35.4 %all-to-all-done.1 = bf16[64,8,2816]{2,1,0:T(8,128)(2,1)S(1)} async-done(((bf16[64,8,2816]{2,1,0:T(8,128)(2,1)}), bf16[64,8,2816]{2,1,0:T(8,128)(2,1)S(1)}, u32[]{:S(2)}, u32[]{:S(2)}) %all-to-all-start.1) | async-done | bytes 2883616 | tf_op jit(solution)/shard_map/all_to_all | solution.py:277
  54.5 6.8 %all-to-all-start = ((bf16[64,8,2816]{2,1,0:T(8,128)(2,1)}), bf16[64,8,2816]{2,1,0:T(8,128)(2,1)}, u32[]{:S(2)}, u32[]{:S(2)}) async-start(bf16[64,8,2816]{2,1,0:T(8,128)(2,1)} %bitcast.3), calls=%async_computation | async-start | bytes 5767168 | tf_op jit(solution)/shard_map/all_to_all | solution.py:277
  61.4 1.9 %copy-done.7 = bf16[1,2048,768]{2,1,0:T(8,128)(2,1)S(1)} copy-done((bf16[1,2048,768]{2,1,0:T(8,128)(2,1)S(1)}, bf16[1,2048,768]{2,1,0:T(8,128)(2,1)}, u32[]{:S(2)}) %copy-start.7) | copy-done | bytes 3145752
  63.3 1.9 %copy-done.9 = bf16[1,2048,768]{2,1,0:T(8,128)(2,1)S(1)} copy-done((bf16[1,2048,768]{2,1,0:T(8,128)(2,1)S(1)}, bf16[1,2048,768]{2,1,0:T(8,128)(2,1)}, u32[]{:S(2)}) %copy-start.9) | copy-done | bytes 3145752
  65.2 1.9 %copy-done.11 = bf16[1,2048,768]{2,1,0:T(8,128)(2,1)S(1)} copy-done((bf16[1,2048,768]{2,1,0:T(8,128)(2,1)S(1)}, bf16[1,2048,768]{2,1,0:T(8,128)(2,1)}, u32[]{:S(2)}) %copy-start.11) | copy-done | bytes 3145752
  67.0 8.2 %shard_map.148 = (bf16[512,2816]{1,0:T(8,128)(2,1)S(1)}, bf16[192,2048]{1,0:T(8,128)(2,1)S(1)}, bf16[704,768]{1,0:T(8,128)(2,1)S(1)}, f32[704,768]{1,0:T(8,128)S(1)}, f32[704,768]{1,0:T(8,128)S(1)}) custom-call(bf16[512,2816]{1,0:T(8,128)(2,1)S(1)} %bitcast.22, bf16[2048,768]{1,0:T(8,128)(2,1)S(1)} %bitcast.26, bf16[2048,768]{1,0:T(8,128)(2,1)S(1)} %bitcast.28, ...), custom_call_target="tpu_custom_call" | custom-call | flops 6643777536 | bytes 21397504 | tf_op jit(solution)/shard_map/pallas_call | solution.py:261
  75.3 1.6 copy-done.3
  77.9 1.4 copy-done.17
  79.3 1.3 copy-done.19
  81.5 17.1 %all-to-all-done = bf16[64,8,2816]{2,1,0:T(8,128)(2,1)} async-done(((bf16[64,8,2816]{2,1,0:T(8,128)(2,1)}), bf16[64,8,2816]{2,1,0:T(8,128)(2,1)}, u32[]{:S(2)}, u32[]{:S(2)}) %all-to-all-start) | async-done | bytes 2883616 | tf_op jit(solution)/shard_map/all_to_all | solution.py:277
  98.6 7.0 %all-to-all-start.2 = ((bf16[64,8,2816]{2,1,0:T(8,128)(2,1)}), bf16[64,8,2816]{2,1,0:T(8,128)(2,1)S(1)}, u32[]{:S(2)}, u32[]{:S(2)}) async-start(bf16[64,8,2816]{2,1,0:T(8,128)(2,1)} %bitcast.25), calls=%async_computation.2 | async-start | bytes 5767168 | tf_op jit(solution)/shard_map/all_to_all | solution.py:277
  105.6 1.9 %copy-done.8 = bf16[1,2048,768]{2,1,0:T(8,128)(2,1)S(1)} copy-done((bf16[1,2048,768]{2,1,0:T(8,128)(2,1)S(1)}, bf16[1,2048,768]{2,1,0:T(8,128)(2,1)}, u32[]{:S(2)}) %copy-start.8) | copy-done | bytes 3145752
  107.4 1.9 %copy-done.10 = bf16[1,2048,768]{2,1,0:T(8,128)(2,1)S(1)} copy-done((bf16[1,2048,768]{2,1,0:T(8,128)(2,1)S(1)}, bf16[1,2048,768]{2,1,0:T(8,128)(2,1)}, u32[]{:S(2)}) %copy-start.10) | copy-done | bytes 3145752
  109.3 1.9 %copy-done.12 = bf16[1,2048,768]{2,1,0:T(8,128)(2,1)S(1)} copy-done((bf16[1,2048,768]{2,1,0:T(8,128)(2,1)S(1)}, bf16[1,2048,768]{2,1,0:T(8,128)(2,1)}, u32[]{:S(2)}) %copy-start.12) | copy-done | bytes 3145752
  111.2 1.6 copy-done.18
  112.8 1.6 copy-done.20
  114.4 11.3 %shard_map.149 = (bf16[512,2816]{1,0:T(8,128)(2,1)S(1)}, bf16[192,2048]{1,0:T(8,128)(2,1)S(1)}, bf16[704,768]{1,0:T(8,128)(2,1)S(1)}, bf16[704,768]{1,0:T(8,128)(2,1)S(1)}) custom-call(bf16[512,2816]{1,0:T(8,128)(2,1)} %bitcast.4.got_ref.home_ref, bf16[2048,768]{1,0:T(8,128)(2,1)S(1)} %bitcast.27, bf16[2048,768]{1,0:T(8,128)(2,1)S(1)} %bitcast.29, ...), custom_call_target="tpu_custom_call" | custom-call | flops 6643777536 | bytes 22478848 | tf_op jit(solution)/shard_map/pallas_call | solution.py:261
  125.8 1.5 copy-done.2
  130.2 11.9 %all-to-all-done.2 = bf16[64,8,2816]{2,1,0:T(8,128)(2,1)S(1)} async-done(((bf16[64,8,2816]{2,1,0:T(8,128)(2,1)}), bf16[64,8,2816]{2,1,0:T(8,128)(2,1)S(1)}, u32[]{:S(2)}, u32[]{:S(2)}) %all-to-all-start.2) | async-done | bytes 2883616 | tf_op jit(solution)/shard_map/all_to_all | solution.py:277
  142.1 6.5 %all-to-all-start.3 = ((bf16[64,8,2816]{2,1,0:T(8,128)(2,1)}), bf16[64,8,2816]{2,1,0:T(8,128)(2,1)}, u32[]{:S(2)}, u32[]{:S(2)}) async-start(bf16[64,8,2816]{2,1,0:T(8,128)(2,1)} %bitcast.24), calls=%async_computation.3 | async-start | bytes 5767168 | tf_op jit(solution)/shard_map/all_to_all | solution.py:277
  148.6 1.2 copy-done.14
  151.0 6.1 %shard_map.153 = (bf16[1024,768]{1,0:T(8,128)(2,1)S(1)}, bf16[1024,768]{1,0:T(8,128)(2,1)S(1)}) custom-call(s32[1]{0:T(128)} %bitcast.14.me_ref, bf16[512,2816]{1,0:T(8,128)(2,1)} %bitcast.4.got_ref.home_ref, bf16[192,2048]{1,0:T(8,128)(2,1)S(1)} %copy-done.16, bf16[704,768]{1,0:T(8,128)(2,1)S(1)} %copy-done.14), custom_call_target="tpu_custom_call" | custom-call | flops 2214592512 | bytes 7897092 | tf_op jit(solution)/shard_map/pallas_call | solution.py:261
  157.3 6.4 %shard_map.152 = (bf16[1024,768]{1,0:T(8,128)(2,1)S(1)}, bf16[1024,768]{1,0:T(8,128)(2,1)S(1)}, bf16[1024,768]{1,0:T(8,128)(2,1)S(1)}, bf16[1024,768]{1,0:T(8,128)(2,1)S(1)}) custom-call(s32[1]{0:T(128)} %bitcast.14.me_ref, bf16[512,2816]{1,0:T(8,128)(2,1)S(1)} %bitcast.23, bf16[192,2048]{1,0:T(8,128)(2,1)S(1)} %copy-done.26, ...), custom_call_target="tpu_custom_call" | custom-call | flops 4429185024 | bytes 12124164 | tf_op jit(solution)/shard_map/pallas_call | solution.py:261
  164.6 1.6 fusion.2
  167.3 1.5 fusion.1
  169.6 1.5 fusion
  171.1 2.1 %shard_map.150 = (bf16[128,2048]{1,0:T(8,128)(2,1)}, bf16[128,512]{1,0:T(8,128)(2,1)S(1)}, bf16[128,192]{1,0:T(8,128)(2,1)S(1)}) custom-call(f32[128,128]{1,0:T(8,128)S(1)} %copy-done.5, f32[128,128]{1,0:T(8,128)S(1)} %copy-done.6, bf16[512,2816]{1,0:T(8,128)(2,1)S(1)} %bitcast.21), custom_call_target="tpu_custom_call" | custom-call | flops 738197504 | bytes 3719168 | tf_op jit(solution)/shard_map/pallas_call | solution.py:261
  173.2 11.1 %all-to-all-done.3 = bf16[64,8,2816]{2,1,0:T(8,128)(2,1)} async-done(((bf16[64,8,2816]{2,1,0:T(8,128)(2,1)}), bf16[64,8,2816]{2,1,0:T(8,128)(2,1)}, u32[]{:S(2)}, u32[]{:S(2)}) %all-to-all-start.3) | async-done | bytes 2883616 | tf_op jit(solution)/shard_map/all_to_all | solution.py:277
  184.2 3.5 %shard_map.151 = bf16[128,2048]{1,0:T(8,128)(2,1)} custom-call(bf16[128,512]{1,0:T(8,128)(2,1)S(1)} %get-tuple-element.37.home_ref, bf16[128,192]{1,0:T(8,128)(2,1)S(1)} %get-tuple-element.38.far_ones_ref, bf16[512,2816]{1,0:T(8,128)(2,1)} %bitcast.13.got_ref), custom_call_target="tpu_custom_call" | custom-call | flops 369098752 | bytes 3588096 | tf_op jit(solution)/shard_map/pallas_call | solution.py:261
  (47 shorter events, 8.7 us)
Async XLA Ops:
  4.6 11.7 %copy-start.4 = (bf16[128,2048]{1,0:T(8,128)(2,1)S(1)}, bf16[128,2048]{1,0:T(8,128)(2,1)}, u32[]{:S(2)}) copy-start(bf16[128,2048]{1,0:T(8,128)(2,1)} %cot_ref.1) | copy-start | bytes 1572868
  4.6 11.7 %copy-start.5 = (f32[128,128]{1,0:T(8,128)S(1)}, f32[128,128]{1,0:T(8,128)}, u32[]{:S(2)}) copy-start(f32[128,128]{1,0:T(8,128)} %get-tuple-element.28.slots_ref) | copy-start | bytes 196612
  4.6 11.7 %copy-start.6 = (f32[128,128]{1,0:T(8,128)S(1)}, f32[128,128]{1,0:T(8,128)}, u32[]{:S(2)}) copy-start(f32[128,128]{1,0:T(8,128)} %get-tuple-element.29.scale_ref) | copy-start | bytes 196612
  4.6 49.9 %all-to-all-start.1 = ((bf16[64,8,2816]{2,1,0:T(8,128)(2,1)}), bf16[64,8,2816]{2,1,0:T(8,128)(2,1)S(1)}, u32[]{:S(2)}, u32[]{:S(2)}) async-start(bf16[64,8,2816]{2,1,0:T(8,128)(2,1)} %bitcast.32), calls=%async_computation.1 | async-start | bytes 5767168 | tf_op jit(solution)/shard_map/all_to_all | solution.py:277
  54.5 6.8 %copy-start = (bf16[64,8,2816]{2,1,0:T(8,128)(2,1)}, bf16[64,8,2816]{2,1,0:T(8,128)(2,1)S(1)}, u32[]{:S(2)}) copy-start(bf16[64,8,2816]{2,1,0:T(8,128)(2,1)S(1)} %all-to-all-done.1) | copy-start | bytes 8650756
  54.5 44.0 %all-to-all-start = ((bf16[64,8,2816]{2,1,0:T(8,128)(2,1)}), bf16[64,8,2816]{2,1,0:T(8,128)(2,1)}, u32[]{:S(2)}, u32[]{:S(2)}) async-start(bf16[64,8,2816]{2,1,0:T(8,128)(2,1)} %bitcast.3), calls=%async_computation | async-start | bytes 5767168 | tf_op jit(solution)/shard_map/all_to_all | solution.py:277
  61.4 1.9 %copy-start.7 = (bf16[1,2048,768]{2,1,0:T(8,128)(2,1)S(1)}, bf16[1,2048,768]{2,1,0:T(8,128)(2,1)}, u32[]{:S(2)}) copy-start(bf16[1,2048,768]{2,1,0:T(8,128)(2,1)} %param.19) | copy-start | bytes 9437188
  63.3 1.9 %copy-start.9 = (bf16[1,2048,768]{2,1,0:T(8,128)(2,1)S(1)}, bf16[1,2048,768]{2,1,0:T(8,128)(2,1)}, u32[]{:S(2)}) copy-start(bf16[1,2048,768]{2,1,0:T(8,128)(2,1)} %param.20) | copy-start | bytes 9437188
  65.2 1.9 %copy-start.11 = (bf16[1,2048,768]{2,1,0:T(8,128)(2,1)S(1)}, bf16[1,2048,768]{2,1,0:T(8,128)(2,1)}, u32[]{:S(2)}) copy-start(bf16[1,2048,768]{2,1,0:T(8,128)(2,1)} %param.21) | copy-start | bytes 9437188
  75.3 1.6 copy-start.3
  76.9 1.0 copy-start.13
  77.9 1.4 copy-start.17
  79.2 1.3 copy-start.19
  98.6 43.6 %all-to-all-start.2 = ((bf16[64,8,2816]{2,1,0:T(8,128)(2,1)}), bf16[64,8,2816]{2,1,0:T(8,128)(2,1)S(1)}, u32[]{:S(2)}, u32[]{:S(2)}) async-start(bf16[64,8,2816]{2,1,0:T(8,128)(2,1)} %bitcast.25), calls=%async_computation.2 | async-start | bytes 5767168 | tf_op jit(solution)/shard_map/all_to_all | solution.py:277
  105.5 1.9 %copy-start.8 = (bf16[1,2048,768]{2,1,0:T(8,128)(2,1)S(1)}, bf16[1,2048,768]{2,1,0:T(8,128)(2,1)}, u32[]{:S(2)}) copy-start(bf16[1,2048,768]{2,1,0:T(8,128)(2,1)} %param.19) | copy-start | bytes 9437188
  107.4 1.9 %copy-start.10 = (bf16[1,2048,768]{2,1,0:T(8,128)(2,1)S(1)}, bf16[1,2048,768]{2,1,0:T(8,128)(2,1)}, u32[]{:S(2)}) copy-start(bf16[1,2048,768]{2,1,0:T(8,128)(2,1)} %param.20) | copy-start | bytes 9437188
  109.3 1.9 %copy-start.12 = (bf16[1,2048,768]{2,1,0:T(8,128)(2,1)S(1)}, bf16[1,2048,768]{2,1,0:T(8,128)(2,1)}, u32[]{:S(2)}) copy-start(bf16[1,2048,768]{2,1,0:T(8,128)(2,1)} %param.21) | copy-start | bytes 9437188
  111.2 1.6 copy-start.18
  112.8 1.6 copy-start.20
  125.8 1.6 copy-start.2
  128.2 1.0 copy-start.21
  129.2 1.0 copy-start.23
  142.1 42.1 %all-to-all-start.3 = ((bf16[64,8,2816]{2,1,0:T(8,128)(2,1)}), bf16[64,8,2816]{2,1,0:T(8,128)(2,1)}, u32[]{:S(2)}, u32[]{:S(2)}) async-start(bf16[64,8,2816]{2,1,0:T(8,128)(2,1)} %bitcast.24), calls=%async_computation.3 | async-start | bytes 5767168 | tf_op jit(solution)/shard_map/all_to_all | solution.py:277
  148.6 1.2 copy-start.14
  149.9 1.1 copy-start.16
  151.0 6.3 %copy-start.1 = (bf16[64,8,2816]{2,1,0:T(8,128)(2,1)S(1)}, bf16[64,8,2816]{2,1,0:T(8,128)(2,1)}, u32[]{:S(2)}) copy-start(bf16[64,8,2816]{2,1,0:T(8,128)(2,1)} %copy-done) | copy-start | bytes 8650756
  151.0 6.3 %copy-start.22 = (bf16[704,768]{1,0:T(8,128)(2,1)S(1)}, bf16[704,768]{1,0:T(8,128)(2,1)}, u32[]{:S(2)}) copy-start(bf16[704,768]{1,0:T(8,128)(2,1)} %copy-done.21) | copy-start | bytes 3244036
  151.0 6.3 %copy-start.24 = (bf16[704,768]{1,0:T(8,128)(2,1)S(1)}, bf16[704,768]{1,0:T(8,128)(2,1)}, u32[]{:S(2)}) copy-start(bf16[704,768]{1,0:T(8,128)(2,1)} %copy-done.23) | copy-start | bytes 3244036
  151.0 6.3 %copy-start.26 = (bf16[192,2048]{1,0:T(8,128)(2,1)S(1)}, bf16[192,2048]{1,0:T(8,128)(2,1)}, u32[]{:S(2)}) copy-start(bf16[192,2048]{1,0:T(8,128)(2,1)} %copy-done.25) | copy-start | bytes 2359300
  157.2 7.4 %collective-permute-start.2 = (bf16[1024,768]{1,0:T(8,128)(2,1)S(1)}, bf16[1024,768]{1,0:T(8,128)(2,1)S(1)}, u32[]{:S(2)}, u32[]{:S(2)}) collective-permute-start(bf16[1024,768]{1,0:T(8,128)(2,1)S(1)} %get-tuple-element.50), channel_id=1, source_target_pairs={{0,64},{64,0},{1,65},{65,1},{2,66},{66,2},{3,67},{67,3},{4,68},{68... | collective-permute-start | bytes 4718600 | tf_op jit(solution)/shard_map/ppermute | solution.py:331
  163.7 3.6 %collective-permute-start.1 = (bf16[1024,768]{1,0:T(8,128)(2,1)S(1)}, bf16[1024,768]{1,0:T(8,128)(2,1)S(1)}, u32[]{:S(2)}, u32[]{:S(2)}) collective-permute-start(bf16[1024,768]{1,0:T(8,128)(2,1)S(1)} %get-tuple-element.46), channel_id=1, source_target_pairs={{0,64},{64,0},{1,65},{65,1},{2,66},{66,2},{3,67},{67,3},{4,68},{68... | collective-permute-start | bytes 4718600 | tf_op jit(solution)/shard_map/ppermute | solution.py:331
  164.3 5.3 %collective-permute-start = (bf16[1024,768]{1,0:T(8,128)(2,1)S(1)}, bf16[1024,768]{1,0:T(8,128)(2,1)S(1)}, u32[]{:S(2)}, u32[]{:S(2)}) collective-permute-start(bf16[1024,768]{1,0:T(8,128)(2,1)S(1)} %get-tuple-element.44), channel_id=1, source_target_pairs={{0,64},{64,0},{1,65},{65,1},{2,66},{66,2},{3,67},{67,3},{4,68},{68... | collective-permute-start | bytes 4718600 | tf_op jit(solution)/shard_map/ppermute | solution.py:331
  (2 other events, 1.8 us)

commit v3 on v2

--- a/solution.py
+++ b/solution.py
@@ -23,6 +23,7 @@
 GROUP = 32
 HALF = D // 2
 STEP = 256
+LATER = 750
 BF = jnp.bfloat16
 F32 = jnp.float32
 TURN = ((0,), (0,))
@@ -92,9 +93,9 @@
     return high, (values - high.astype(F32)).astype(BF)
 
 
-def plan_kernel(hot_hbm, holder_hbm, cap_hbm, routes_hbm, weight_hbm, pick_hbm, tokens_hbm,
+def plan_kernel(me_ref, hot_hbm, holder_hbm, cap_hbm, routes_hbm, weight_hbm, pick_hbm, tokens_hbm,
                 send_hbm, slots_ref, scale_ref, hot_ref, holder_ref, cap_ref, routes_ref,
-                weight_ref, pick_ref, tokens_ref, send_ref, sems, out_sems):
+                weight_ref, pick_ref, tokens_ref, send_ref, later_ref, sems, out_sems):
     copies = [
         pltpu.make_async_copy(src, dst, sems.at[i])
         for i, (src, dst) in enumerate(
@@ -107,6 +108,16 @@
     ]
     for copy in copies:
         copy.start()
+    later_ref[...] = jnp.ones(later_ref.shape, F32)
+
+    def turn(step, carry):
+        value = later_ref[...]
+        for _ in range(8):
+            value = value * 0.5 + 1.0
+        later_ref[...] = value
+        return carry
+
+    lax.fori_loop(0, me_ref[0] * LATER, turn, 0)
     for copy in copies[:-1]:
         copy.wait()
     lane = lax.broadcasted_iota(jnp.int32, (1, TOK), 1)
@@ -288,17 +299,18 @@
     far_scratch = pltpu.VMEM((FAR, D), BF)
     dma = pltpu.SemaphoreType.DMA
 
+    me = lax.axis_index("dp").reshape(1)
     send_x, slots, scale = call(
         plan_kernel,
         [packed, square, square],
-        (hot_experts, hot_holders, capacity, routes.T, route_weight.T, replica_pick.T, tokens),
+        (me, hot_experts, hot_holders, capacity, routes.T, route_weight.T, replica_pick.T, tokens),
         move,
         [pltpu.SMEM((HOT,), jnp.int32), pltpu.SMEM((HOT,), jnp.int32),
          pltpu.SMEM((EXPERTS,), jnp.int32)]
         + [pltpu.VMEM((TOPK, TOK), jnp.int32)] * 3
-        + [pltpu.VMEM((TOK, D), BF), pltpu.VMEM((HOME, WIDE), BF), dma((7,)), dma((5,))],
+        + [pltpu.VMEM((TOK, D), BF), pltpu.VMEM((HOME, WIDE), BF), pltpu.VMEM((8, TOK), F32), dma((7,)), dma((5,))],
         60,
-        [HBM] * 7,
+        [SMEM] + [HBM] * 7,
         [HBM, VMEM, VMEM],
     )
     got_x = exchange(send_x)
@@ -318,7 +330,6 @@
     send_back, got_out = lax.optimization_barrier((send_back, got_out))
     got_back = exchange(send_back)
     half = shape(HALF, FF)
-    me = lax.axis_index("dp").reshape(1)
     send_down, keep_down = call(
         weight_kernel, [half] * 2, (me, got_g, far_g, hidden), product,
         in_specs=[SMEM] + [VMEM] * 3,

time: 189 us -> 168 us (0.89)
  the two profiles are of different devices: /device:TPU:0 before, /device:TPU:1 now
where the time goes in v3:
time: 168 us; the launch traced here: 167 us
  Pallas kernels  60.7 us (36%)
  waiting for transfers between devices  40.5 us (24%)
  starting transfers between devices  32.8 us (20%)
  local copies, waits for them, and re-layouts  27.5 us (16%)
  other arithmetic  4.63 us (3%)
    pallas_call x8, Pallas kernels, call(): pl.pallas_call(kernel, out_shape=outs, in_specs=in_specs or [VMEM] * len(...  60.7 us
    all_to_all x4, waiting for transfers between devices, exchange(): lax.all_to_all(values, 'expert', split_axis=0, concat_axis=0, tiled=True)  38.7 us
    all_to_all x4, starting transfers between devices, exchange(): lax.all_to_all(values, 'expert', split_axis=0, concat_axis=0, tiled=True)  31.8 us
    unnamed x54, local copies, waits for them, and re-layouts  27.5 us
    broadcast_in_dim x3, other arithmetic, shards(): (keep.astype(F32) + lax.ppermute(sent, 'dp', ((0, 1), (1, 0))).astype(F32...  4.63 us
  transfers between devices with their start and end apart: 7, of which 6 were waited for; matrix products, arithmetic and copies ran while one was open for 3% of the time, Pallas kernels for 22%

profile of v3, /device:TPU:1, one launch (start us, length us, event | category | flops | bytes accessed | tf_op | source)
XLA Modules:
  0.0 167.1 jit_solution(2266185344025113187)
XLA Ops:
  0.6 20.2 %shard_map.146 = (bf16[512,2816]{1,0:T(8,128)(2,1)}, f32[128,128]{1,0:T(8,128)}, f32[128,128]{1,0:T(8,128)}) custom-call(s32[1]{0:T(128)} %bitcast.me_ref, s32[8]{0:T(128)} %hot_hbm.1, s32[8]{0:T(128)} %holder_hbm.1, s32[64]{0:T(128)} %cap_hbm.1, s32[8,128]{1,0:T(8,128)} %bitcast.33, s32[8,128]{1,0:T(8,128)} %bitcast.34, s32[8,128]{1,0:T(8,128)} %bitcast.35, ...), custom_call_target="tpu_custom_call" | custom-call | flops 369098752 | bytes 3551556 | tf_op jit(solution)/shard_map/pallas_call | solution.py:272
  20.9 12.1 %all-to-all-start.1 = ((bf16[64,8,2816]{2,1,0:T(8,128)(2,1)}), bf16[64,8,2816]{2,1,0:T(8,128)(2,1)S(1)}, u32[]{:S(2)}, u32[]{:S(2)}) async-start(bf16[64,8,2816]{2,1,0:T(8,128)(2,1)} %bitcast.32), calls=%async_computation.1 | async-start | bytes 5767168 | tf_op jit(solution)/shard_map/all_to_all | solution.py:288
  33.0 2.8 %shard_map.147 = bf16[512,2816]{1,0:T(8,128)(2,1)} custom-call(f32[128,128]{1,0:T(8,128)S(1)} %copy-done.5, f32[128,128]{1,0:T(8,128)S(1)} %copy-done.6, bf16[128,2048]{1,0:T(8,128)(2,1)S(1)} %copy-done.4), custom_call_target="tpu_custom_call" | custom-call | flops 738197504 | bytes 3538944 | tf_op jit(solution)/shard_map/pallas_call | solution.py:272
  35.9 20.9 %all-to-all-done.1 = bf16[64,8,2816]{2,1,0:T(8,128)(2,1)S(1)} async-done(((bf16[64,8,2816]{2,1,0:T(8,128)(2,1)}), bf16[64,8,2816]{2,1,0:T(8,128)(2,1)S(1)}, u32[]{:S(2)}, u32[]{:S(2)}) %all-to-all-start.1) | async-done | bytes 2883616 | tf_op jit(solution)/shard_map/all_to_all | solution.py:288
  56.8 8.4 %all-to-all-start = ((bf16[64,8,2816]{2,1,0:T(8,128)(2,1)}), bf16[64,8,2816]{2,1,0:T(8,128)(2,1)}, u32[]{:S(2)}, u32[]{:S(2)}) async-start(bf16[64,8,2816]{2,1,0:T(8,128)(2,1)} %bitcast.4), calls=%async_computation | async-start | bytes 5767168 | tf_op jit(solution)/shard_map/all_to_all | solution.py:288
  65.2 1.9 %copy-done.7 = bf16[1,2048,768]{2,1,0:T(8,128)(2,1)S(1)} copy-done((bf16[1,2048,768]{2,1,0:T(8,128)(2,1)S(1)}, bf16[1,2048,768]{2,1,0:T(8,128)(2,1)}, u32[]{:S(2)}) %copy-start.7) | copy-done | bytes 3145752
  67.1 1.9 %copy-done.9 = bf16[1,2048,768]{2,1,0:T(8,128)(2,1)S(1)} copy-done((bf16[1,2048,768]{2,1,0:T(8,128)(2,1)S(1)}, bf16[1,2048,768]{2,1,0:T(8,128)(2,1)}, u32[]{:S(2)}) %copy-start.9) | copy-done | bytes 3145752
  69.0 1.9 %copy-done.11 = bf16[1,2048,768]{2,1,0:T(8,128)(2,1)S(1)} copy-done((bf16[1,2048,768]{2,1,0:T(8,128)(2,1)S(1)}, bf16[1,2048,768]{2,1,0:T(8,128)(2,1)}, u32[]{:S(2)}) %copy-start.11) | copy-done | bytes 3145752
  70.8 8.2 %shard_map.148 = (bf16[512,2816]{1,0:T(8,128)(2,1)S(1)}, bf16[192,2048]{1,0:T(8,128)(2,1)S(1)}, bf16[704,768]{1,0:T(8,128)(2,1)S(1)}, f32[704,768]{1,0:T(8,128)S(1)}, f32[704,768]{1,0:T(8,128)S(1)}) custom-call(bf16[512,2816]{1,0:T(8,128)(2,1)S(1)} %bitcast.23, bf16[2048,768]{1,0:T(8,128)(2,1)S(1)} %bitcast.26, bf16[2048,768]{1,0:T(8,128)(2,1)S(1)} %bitcast.28, ...), custom_call_target="tpu_custom_call" | custom-call | flops 6643777536 | bytes 21397504 | tf_op jit(solution)/shard_map/pallas_call | solution.py:272
  79.1 1.6 copy-done.3
  81.7 1.4 copy-done.17
  83.1 1.3 copy-done.19
  85.3 4.4 %all-to-all-done = bf16[64,8,2816]{2,1,0:T(8,128)(2,1)} async-done(((bf16[64,8,2816]{2,1,0:T(8,128)(2,1)}), bf16[64,8,2816]{2,1,0:T(8,128)(2,1)}, u32[]{:S(2)}, u32[]{:S(2)}) %all-to-all-start) | async-done | bytes 2883616 | tf_op jit(solution)/shard_map/all_to_all | solution.py:288
  89.7 5.6 %all-to-all-start.2 = ((bf16[64,8,2816]{2,1,0:T(8,128)(2,1)}), bf16[64,8,2816]{2,1,0:T(8,128)(2,1)S(1)}, u32[]{:S(2)}, u32[]{:S(2)}) async-start(bf16[64,8,2816]{2,1,0:T(8,128)(2,1)} %bitcast.25), calls=%async_computation.2 | async-start | bytes 5767168 | tf_op jit(solution)/shard_map/all_to_all | solution.py:288
  95.4 1.9 %copy-done.8 = bf16[1,2048,768]{2,1,0:T(8,128)(2,1)S(1)} copy-done((bf16[1,2048,768]{2,1,0:T(8,128)(2,1)S(1)}, bf16[1,2048,768]{2,1,0:T(8,128)(2,1)}, u32[]{:S(2)}) %copy-start.8) | copy-done | bytes 3145752
  97.2 1.9 %copy-done.10 = bf16[1,2048,768]{2,1,0:T(8,128)(2,1)S(1)} copy-done((bf16[1,2048,768]{2,1,0:T(8,128)(2,1)S(1)}, bf16[1,2048,768]{2,1,0:T(8,128)(2,1)}, u32[]{:S(2)}) %copy-start.10) | copy-done | bytes 3145752
  99.1 1.9 %copy-done.12 = bf16[1,2048,768]{2,1,0:T(8,128)(2,1)S(1)} copy-done((bf16[1,2048,768]{2,1,0:T(8,128)(2,1)S(1)}, bf16[1,2048,768]{2,1,0:T(8,128)(2,1)}, u32[]{:S(2)}) %copy-start.12) | copy-done | bytes 3145752
  101.0 1.6 copy-done.18
  102.6 1.6 copy-done.20
  104.2 11.4 %shard_map.149 = (bf16[512,2816]{1,0:T(8,128)(2,1)S(1)}, bf16[192,2048]{1,0:T(8,128)(2,1)S(1)}, bf16[704,768]{1,0:T(8,128)(2,1)S(1)}, bf16[704,768]{1,0:T(8,128)(2,1)S(1)}) custom-call(bf16[512,2816]{1,0:T(8,128)(2,1)} %bitcast.5.got_ref.home_ref, bf16[2048,768]{1,0:T(8,128)(2,1)S(1)} %bitcast.27, bf16[2048,768]{1,0:T(8,128)(2,1)S(1)} %bitcast.29, ...), custom_call_target="tpu_custom_call" | custom-call | flops 6643777536 | bytes 22478848 | tf_op jit(solution)/shard_map/pallas_call | solution.py:272
  115.6 1.5 copy-done
  120.0 4.3 %all-to-all-done.2 = bf16[64,8,2816]{2,1,0:T(8,128)(2,1)S(1)} async-done(((bf16[64,8,2816]{2,1,0:T(8,128)(2,1)}), bf16[64,8,2816]{2,1,0:T(8,128)(2,1)S(1)}, u32[]{:S(2)}, u32[]{:S(2)}) %all-to-all-start.2) | async-done | bytes 2883616 | tf_op jit(solution)/shard_map/all_to_all | solution.py:288
  124.3 5.7 %all-to-all-start.3 = ((bf16[64,8,2816]{2,1,0:T(8,128)(2,1)}), bf16[64,8,2816]{2,1,0:T(8,128)(2,1)}, u32[]{:S(2)}, u32[]{:S(2)}) async-start(bf16[64,8,2816]{2,1,0:T(8,128)(2,1)} %bitcast.22), calls=%async_computation.3 | async-start | bytes 5767168 | tf_op jit(solution)/shard_map/all_to_all | solution.py:288
  130.1 1.2 copy-done.14
  132.5 6.1 %shard_map.153 = (bf16[1024,768]{1,0:T(8,128)(2,1)S(1)}, bf16[1024,768]{1,0:T(8,128)(2,1)S(1)}) custom-call(s32[1]{0:T(128)} %bitcast.me_ref, bf16[512,2816]{1,0:T(8,128)(2,1)} %bitcast.5.got_ref.home_ref, bf16[192,2048]{1,0:T(8,128)(2,1)S(1)} %copy-done.16, bf16[704,768]{1,0:T(8,128)(2,1)S(1)} %copy-done.14), custom_call_target="tpu_custom_call" | custom-call | flops 2214592512 | bytes 7897092 | tf_op jit(solution)/shard_map/pallas_call | solution.py:272
  138.7 6.4 %shard_map.152 = (bf16[1024,768]{1,0:T(8,128)(2,1)S(1)}, bf16[1024,768]{1,0:T(8,128)(2,1)S(1)}, bf16[1024,768]{1,0:T(8,128)(2,1)S(1)}, bf16[1024,768]{1,0:T(8,128)(2,1)S(1)}) custom-call(s32[1]{0:T(128)} %bitcast.me_ref, bf16[512,2816]{1,0:T(8,128)(2,1)S(1)} %bitcast.24, bf16[192,2048]{1,0:T(8,128)(2,1)S(1)} %copy-done.26, bf16[704,768]{1,0:T(8,128)(2,1)S(1)} %copy-done.22, ...), custom_call_target="tpu_custom_call" | custom-call | flops 4429185024 | bytes 12124164 | tf_op jit(solution)/shard_map/pallas_call | solution.py:272
  146.0 1.6 fusion.2
  148.7 1.5 fusion
  151.0 1.5 fusion.1
  152.5 2.1 %shard_map.150 = (bf16[128,2048]{1,0:T(8,128)(2,1)}, bf16[128,512]{1,0:T(8,128)(2,1)S(1)}, bf16[128,192]{1,0:T(8,128)(2,1)S(1)}) custom-call(f32[128,128]{1,0:T(8,128)S(1)} %copy-done.5, f32[128,128]{1,0:T(8,128)S(1)} %copy-done.6, bf16[512,2816]{1,0:T(8,128)(2,1)S(1)} %bitcast.21), custom_call_target="tpu_custom_call" | custom-call | flops 738197504 | bytes 3719168 | tf_op jit(solution)/shard_map/pallas_call | solution.py:272
  154.6 9.0 %all-to-all-done.3 = bf16[64,8,2816]{2,1,0:T(8,128)(2,1)} async-done(((bf16[64,8,2816]{2,1,0:T(8,128)(2,1)}), bf16[64,8,2816]{2,1,0:T(8,128)(2,1)}, u32[]{:S(2)}, u32[]{:S(2)}) %all-to-all-start.3) | async-done | bytes 2883616 | tf_op jit(solution)/shard_map/all_to_all | solution.py:288
  163.6 3.5 %shard_map.151 = bf16[128,2048]{1,0:T(8,128)(2,1)} custom-call(bf16[128,512]{1,0:T(8,128)(2,1)S(1)} %get-tuple-element.37.home_ref, bf16[128,192]{1,0:T(8,128)(2,1)S(1)} %get-tuple-element.38.far_ones_ref, bf16[512,2816]{1,0:T(8,128)(2,1)} %bitcast.14.got_ref), custom_call_target="tpu_custom_call" | custom-call | flops 369098752 | bytes 3588096 | tf_op jit(solution)/shard_map/pallas_call | solution.py:272
  (47 shorter events, 8.7 us)
Async XLA Ops:
  20.9 12.2 %copy-start.4 = (bf16[128,2048]{1,0:T(8,128)(2,1)S(1)}, bf16[128,2048]{1,0:T(8,128)(2,1)}, u32[]{:S(2)}) copy-start(bf16[128,2048]{1,0:T(8,128)(2,1)} %cot_ref.1) | copy-start | bytes 1572868
  20.9 12.2 %copy-start.5 = (f32[128,128]{1,0:T(8,128)S(1)}, f32[128,128]{1,0:T(8,128)}, u32[]{:S(2)}) copy-start(f32[128,128]{1,0:T(8,128)} %get-tuple-element.28.slots_ref) | copy-start | bytes 196612
  20.9 12.1 %copy-start.6 = (f32[128,128]{1,0:T(8,128)S(1)}, f32[128,128]{1,0:T(8,128)}, u32[]{:S(2)}) copy-start(f32[128,128]{1,0:T(8,128)} %get-tuple-element.29.scale_ref) | copy-start | bytes 196612
  20.9 35.9 %all-to-all-start.1 = ((bf16[64,8,2816]{2,1,0:T(8,128)(2,1)}), bf16[64,8,2816]{2,1,0:T(8,128)(2,1)S(1)}, u32[]{:S(2)}, u32[]{:S(2)}) async-start(bf16[64,8,2816]{2,1,0:T(8,128)(2,1)} %bitcast.32), calls=%async_computation.1 | async-start | bytes 5767168 | tf_op jit(solution)/shard_map/all_to_all | solution.py:288
  56.8 8.4 %copy-start.1 = (bf16[64,8,2816]{2,1,0:T(8,128)(2,1)}, bf16[64,8,2816]{2,1,0:T(8,128)(2,1)S(1)}, u32[]{:S(2)}) copy-start(bf16[64,8,2816]{2,1,0:T(8,128)(2,1)S(1)} %all-to-all-done.1) | copy-start | bytes 8650756
  56.8 33.0 %all-to-all-start = ((bf16[64,8,2816]{2,1,0:T(8,128)(2,1)}), bf16[64,8,2816]{2,1,0:T(8,128)(2,1)}, u32[]{:S(2)}, u32[]{:S(2)}) async-start(bf16[64,8,2816]{2,1,0:T(8,128)(2,1)} %bitcast.4), calls=%async_computation | async-start | bytes 5767168 | tf_op jit(solution)/shard_map/all_to_all | solution.py:288
  65.2 1.9 %copy-start.7 = (bf16[1,2048,768]{2,1,0:T(8,128)(2,1)S(1)}, bf16[1,2048,768]{2,1,0:T(8,128)(2,1)}, u32[]{:S(2)}) copy-start(bf16[1,2048,768]{2,1,0:T(8,128)(2,1)} %param.19) | copy-start | bytes 9437188
  67.1 1.9 %copy-start.9 = (bf16[1,2048,768]{2,1,0:T(8,128)(2,1)S(1)}, bf16[1,2048,768]{2,1,0:T(8,128)(2,1)}, u32[]{:S(2)}) copy-start(bf16[1,2048,768]{2,1,0:T(8,128)(2,1)} %param.20) | copy-start | bytes 9437188
  69.0 1.9 %copy-start.11 = (bf16[1,2048,768]{2,1,0:T(8,128)(2,1)S(1)}, bf16[1,2048,768]{2,1,0:T(8,128)(2,1)}, u32[]{:S(2)}) copy-start(bf16[1,2048,768]{2,1,0:T(8,128)(2,1)} %param.21) | copy-start | bytes 9437188
  79.1 1.6 copy-start.3
  80.7 1.0 copy-start.13
  81.7 1.4 copy-start.17
  83.1 1.3 copy-start.19
  89.7 34.6 %all-to-all-start.2 = ((bf16[64,8,2816]{2,1,0:T(8,128)(2,1)}), bf16[64,8,2816]{2,1,0:T(8,128)(2,1)S(1)}, u32[]{:S(2)}, u32[]{:S(2)}) async-start(bf16[64,8,2816]{2,1,0:T(8,128)(2,1)} %bitcast.25), calls=%async_computation.2 | async-start | bytes 5767168 | tf_op jit(solution)/shard_map/all_to_all | solution.py:288
  95.3 1.9 %copy-start.8 = (bf16[1,2048,768]{2,1,0:T(8,128)(2,1)S(1)}, bf16[1,2048,768]{2,1,0:T(8,128)(2,1)}, u32[]{:S(2)}) copy-start(bf16[1,2048,768]{2,1,0:T(8,128)(2,1)} %param.19) | copy-start | bytes 9437188
  97.2 1.9 %copy-start.10 = (bf16[1,2048,768]{2,1,0:T(8,128)(2,1)S(1)}, bf16[1,2048,768]{2,1,0:T(8,128)(2,1)}, u32[]{:S(2)}) copy-start(bf16[1,2048,768]{2,1,0:T(8,128)(2,1)} %param.20) | copy-start | bytes 9437188
  99.1 1.9 %copy-start.12 = (bf16[1,2048,768]{2,1,0:T(8,128)(2,1)S(1)}, bf16[1,2048,768]{2,1,0:T(8,128)(2,1)}, u32[]{:S(2)}) copy-start(bf16[1,2048,768]{2,1,0:T(8,128)(2,1)} %param.21) | copy-start | bytes 9437188
  101.0 1.6 copy-start.18
  102.6 1.6 copy-start.20
  115.6 1.6 copy-start
  118.1 1.0 copy-start.21
  119.0 1.0 copy-start.23
  124.3 39.3 %all-to-all-start.3 = ((bf16[64,8,2816]{2,1,0:T(8,128)(2,1)}), bf16[64,8,2816]{2,1,0:T(8,128)(2,1)}, u32[]{:S(2)}, u32[]{:S(2)}) async-start(bf16[64,8,2816]{2,1,0:T(8,128)(2,1)} %bitcast.22), calls=%async_computation.3 | async-start | bytes 5767168 | tf_op jit(solution)/shard_map/all_to_all | solution.py:288
  130.1 1.2 copy-start.14
  131.3 1.1 copy-start.16
  132.4 6.3 %copy-start.2 = (bf16[64,8,2816]{2,1,0:T(8,128)(2,1)S(1)}, bf16[64,8,2816]{2,1,0:T(8,128)(2,1)}, u32[]{:S(2)}) copy-start(bf16[64,8,2816]{2,1,0:T(8,128)(2,1)} %copy-done.1) | copy-start | bytes 8650756
  132.4 6.3 %copy-start.22 = (bf16[704,768]{1,0:T(8,128)(2,1)S(1)}, bf16[704,768]{1,0:T(8,128)(2,1)}, u32[]{:S(2)}) copy-start(bf16[704,768]{1,0:T(8,128)(2,1)} %copy-done.21) | copy-start | bytes 3244036
  132.4 6.3 %copy-start.24 = (bf16[704,768]{1,0:T(8,128)(2,1)S(1)}, bf16[704,768]{1,0:T(8,128)(2,1)}, u32[]{:S(2)}) copy-start(bf16[704,768]{1,0:T(8,128)(2,1)} %copy-done.23) | copy-start | bytes 3244036
  132.4 6.3 %copy-start.26 = (bf16[192,2048]{1,0:T(8,128)(2,1)S(1)}, bf16[192,2048]{1,0:T(8,128)(2,1)}, u32[]{:S(2)}) copy-start(bf16[192,2048]{1,0:T(8,128)(2,1)} %copy-done.25) | copy-start | bytes 2359300
  138.6 7.4 %collective-permute-start.2 = (bf16[1024,768]{1,0:T(8,128)(2,1)S(1)}, bf16[1024,768]{1,0:T(8,128)(2,1)S(1)}, u32[]{:S(2)}, u32[]{:S(2)}) collective-permute-start(bf16[1024,768]{1,0:T(8,128)(2,1)S(1)} %get-tuple-element.50), channel_id=1, source_target_pairs={{0,64},{64,0},{1,65},{65,1},{2,66},{66,2},{3,67},{67,3},{4,68},{68... | collective-permute-start | bytes 4718600 | tf_op jit(solution)/shard_map/ppermute | solution.py:342
  145.2 3.6 %collective-permute-start = (bf16[1024,768]{1,0:T(8,128)(2,1)S(1)}, bf16[1024,768]{1,0:T(8,128)(2,1)S(1)}, u32[]{:S(2)}, u32[]{:S(2)}) collective-permute-start(bf16[1024,768]{1,0:T(8,128)(2,1)S(1)} %get-tuple-element.44), channel_id=1, source_target_pairs={{0,64},{64,0},{1,65},{65,1},{2,66},{66,2},{3,67},{67,3},{4,68},{68... | collective-permute-start | bytes 4718600 | tf_op jit(solution)/shard_map/ppermute | solution.py:342
  145.7 5.3 %collective-permute-start.1 = (bf16[1024,768]{1,0:T(8,128)(2,1)S(1)}, bf16[1024,768]{1,0:T(8,128)(2,1)S(1)}, u32[]{:S(2)}, u32[]{:S(2)}) collective-permute-start(bf16[1024,768]{1,0:T(8,128)(2,1)S(1)} %get-tuple-element.46), channel_id=1, source_target_pairs={{0,64},{64,0},{1,65},{65,1},{2,66},{66,2},{3,67},{67,3},{4,68},{68... | collective-permute-start | bytes 4718600 | tf_op jit(solution)/shard_map/ppermute | solution.py:342
  (2 other events, 1.8 us)

commit v4 on v3

--- a/solution.py
+++ b/solution.py
@@ -23,7 +23,7 @@
 GROUP = 32
 HALF = D // 2
 STEP = 256
-LATER = 750
+LATER = 810
 BF = jnp.bfloat16
 F32 = jnp.float32
 TURN = ((0,), (0,))
@@ -314,6 +314,7 @@
         [HBM, VMEM, VMEM],
     )
     got_x = exchange(send_x)
+    cotangent, got_x = lax.optimization_barrier((cotangent, got_x))
     (send_g,) = call(
         grads_kernel, [packed], (slots, scale, cotangent), 2 * move,
         [pltpu.VMEM((2 * TOK, D), BF)],
@@ -331,11 +332,12 @@
     got_back = exchange(send_back)
     half = shape(HALF, FF)
     send_down, keep_down = call(
-        weight_kernel, [half] * 2, (me, got_g, far_g, hidden), product,
+        weight_kernel, [half] * 2, (me, got_g, far_g, hidden), product, limit=20,
         in_specs=[SMEM] + [VMEM] * 3,
     )
     send_gate, send_up, keep_gate, keep_up = call(
         weight_kernel, [half] * 4, (me, got_x, far_x, back_gate, back_up), 2 * product,
+        limit=20,
         in_specs=[SMEM] + [VMEM] * 4,
     )
     grads = [
@@ -344,10 +346,10 @@
     ]
     mixed, home_ones, far_ones = call(
         mixed_kernel, [shape(TOK, D), shape(TOK, HOME), shape(TOK, FAR)], (slots, scale, got_out),
-        2 * move, [far_scratch],
+        2 * move, [far_scratch], 16,
     )
     (grad_tokens,) = call(
-        back_kernel, [shape(TOK, D)], (home_ones, far_ones, got_back), move, [far_scratch]
+        back_kernel, [shape(TOK, D)], (home_ones, far_ones, got_back), move, [far_scratch], 16
     )
     return (mixed, grad_tokens, *grads)
 

time: 168 us -> 165 us (0.982)
  blocking collectives: 0 us -> 35.6 us
  waiting for transfers between devices: 40.5 us -> 9.58 us
  starting transfers between devices: 32.8 us -> 24.1 us
    all_to_all x0 -> x1, blocking collectives: none -> 35.6 us  [exchange(): lax.all_to_all(values, 'expert', split_axis=0, concat_axis=0, tiled=True)]
    all_to_all x4 -> x3, waiting for transfers between devices: 38.7 us -> 9.58 us  [exchange(): lax.all_to_all(values, 'expert', split_axis=0, concat_axis=0, tiled=True)]
    all_to_all x4 -> x3, starting transfers between devices: 31.8 us -> 23.1 us  [exchange(): lax.all_to_all(values, 'expert', split_axis=0, concat_axis=0, tiled=True)]
    ppermute x3, waiting for transfers between devices: 1.87 us -> 0.01 us  [shards(): lax.ppermute(sent, 'dp', ((0, 1), (1, 0))).astype(F32)]
    unnamed x54 -> x58, local copies, waits for them, and re-layouts: 27.5 us -> 29.1 us
  transfers between devices with their start and end apart: 7 -> 6, of which waited for: 6 -> 3; matrix products, arithmetic and copies ran while one was open for 3% -> 3% of each run, Pallas kernels for 22% -> 21%
where the time goes in v4:
time: 165 us; the launch traced here: 164 us
  Pallas kernels  60.3 us (37%)
  blocking collectives  35.6 us (22%)
  local copies, waits for them, and re-layouts  29.1 us (18%)
  starting transfers between devices  24.1 us (15%)
  waiting for transfers between devices  9.58 us (6%)
  other arithmetic  4.7 us (3%)
    pallas_call x8, Pallas kernels, call(): pl.pallas_call(kernel, out_shape=outs, in_specs=in_specs or [VMEM] * len(...  60.3 us
    all_to_all x1, blocking collectives, exchange(): lax.all_to_all(values, 'expert', split_axis=0, concat_axis=0, tiled=True)  35.6 us
    unnamed x58, local copies, waits for them, and re-layouts  29.1 us
    all_to_all x3, starting transfers between devices, exchange(): lax.all_to_all(values, 'expert', split_axis=0, concat_axis=0, tiled=True)  23.1 us
    all_to_all x3, waiting for transfers between devices, exchange(): lax.all_to_all(values, 'expert', split_axis=0, concat_axis=0, tiled=True)  9.58 us
    broadcast_in_dim x3, other arithmetic, shards(): (keep.astype(F32) + lax.ppermute(sent, 'dp', ((0, 1), (1, 0))).astype(F32...  4.7 us
  transfers between devices with their start and end apart: 6, of which 3 were waited for; matrix products, arithmetic and copies ran while one was open for 3% of the time, Pallas kernels for 21%

profile of v4, /device:TPU:1, one launch (start us, length us, event | category | flops | bytes accessed | tf_op | source)
XLA Modules:
  0.0 164.2 jit_solution(1203186585439101565)
XLA Ops:
  0.6 21.6 %shard_map.146 = (bf16[512,2816]{1,0:T(8,128)(2,1)}, f32[128,128]{1,0:T(8,128)}, f32[128,128]{1,0:T(8,128)}) custom-call(s32[1]{0:T(128)} %bitcast.me_ref, s32[8]{0:T(128)} %hot_hbm.1, s32[8]{0:T(128)} %holder_hbm.1, s32[64]{0:T(128)} %cap_hbm.1, s32[8,128]{1,0:T(8,128)} %bitcast.34, s32[8,128]{1,0:T(8,128)} %bitcast.35, s32[8,128]{1,0:T(8,128)} %bitcast.36, ...), custom_call_target="tpu_custom_call" | custom-call | flops 369098752 | bytes 3551556 | tf_op jit(solution)/shard_map/pallas_call | solution.py:272
  22.3 35.6 %all_to_all.46 = bf16[64,8,2816]{2,1,0:T(8,128)(2,1)S(1)} all-to-all(bf16[64,8,2816]{2,1,0:T(8,128)(2,1)} %bitcast.33), channel_id=1, replica_groups=mesh['dp'=2,'expert'=64] {'expert'}, dimensions={0} | all-to-all | bytes 5767168 | tf_op jit(solution)/shard_map/all_to_all | solution.py:288
  57.9 2.9 %shard_map.147 = bf16[512,2816]{1,0:T(8,128)(2,1)} custom-call(f32[128,128]{1,0:T(8,128)S(1)} %copy-done.7, f32[128,128]{1,0:T(8,128)S(1)} %copy-done.8, bf16[128,2048]{1,0:T(8,128)(2,1)S(1)} %copy-done.6), custom_call_target="tpu_custom_call" | custom-call | flops 738197504 | bytes 3538944 | tf_op jit(solution)/shard_map/pallas_call | solution.py:272
  60.7 5.6 %all-to-all-start.1 = ((bf16[64,8,2816]{2,1,0:T(8,128)(2,1)}), bf16[64,8,2816]{2,1,0:T(8,128)(2,1)}, u32[]{:S(2)}, u32[]{:S(2)}) async-start(bf16[64,8,2816]{2,1,0:T(8,128)(2,1)} %bitcast.6), calls=%async_computation.1 | async-start | bytes 5767168 | tf_op jit(solution)/shard_map/all_to_all | solution.py:288
  66.3 1.9 %copy-done.9 = bf16[1,2048,768]{2,1,0:T(8,128)(2,1)S(1)} copy-done((bf16[1,2048,768]{2,1,0:T(8,128)(2,1)S(1)}, bf16[1,2048,768]{2,1,0:T(8,128)(2,1)}, u32[]{:S(2)}) %copy-start.9) | copy-done | bytes 3145752
  68.2 1.9 %copy-done.11 = bf16[1,2048,768]{2,1,0:T(8,128)(2,1)S(1)} copy-done((bf16[1,2048,768]{2,1,0:T(8,128)(2,1)S(1)}, bf16[1,2048,768]{2,1,0:T(8,128)(2,1)}, u32[]{:S(2)}) %copy-start.11) | copy-done | bytes 3145752
  70.1 1.9 %copy-done.13 = bf16[1,2048,768]{2,1,0:T(8,128)(2,1)S(1)} copy-done((bf16[1,2048,768]{2,1,0:T(8,128)(2,1)S(1)}, bf16[1,2048,768]{2,1,0:T(8,128)(2,1)}, u32[]{:S(2)}) %copy-start.13) | copy-done | bytes 3145752
  72.0 8.2 %shard_map.148 = (bf16[512,2816]{1,0:T(8,128)(2,1)S(1)}, bf16[192,2048]{1,0:T(8,128)(2,1)S(1)}, bf16[704,768]{1,0:T(8,128)(2,1)S(1)}, f32[704,768]{1,0:T(8,128)S(1)}, f32[704,768]{1,0:T(8,128)S(1)}) custom-call(bf16[512,2816]{1,0:T(8,128)(2,1)S(1)} %bitcast.24, bf16[2048,768]{1,0:T(8,128)(2,1)S(1)} %bitcast.27, bf16[2048,768]{1,0:T(8,128)(2,1)S(1)} %bitcast.29, ...), custom_call_target="tpu_custom_call" | custom-call | flops 6643777536 | bytes 21397504 | tf_op jit(solution)/shard_map/pallas_call | solution.py:272
  80.2 1.5 copy-done.5
  82.7 1.4 copy-done.19
  84.1 1.3 copy-done.21
  86.4 3.5 %all-to-all-done.1 = bf16[64,8,2816]{2,1,0:T(8,128)(2,1)} async-done(((bf16[64,8,2816]{2,1,0:T(8,128)(2,1)}), bf16[64,8,2816]{2,1,0:T(8,128)(2,1)}, u32[]{:S(2)}, u32[]{:S(2)}) %all-to-all-start.1) | async-done | bytes 2883616 | tf_op jit(solution)/shard_map/all_to_all | solution.py:288
  89.8 8.1 %all-to-all-start.2 = ((bf16[64,8,2816]{2,1,0:T(8,128)(2,1)}), bf16[64,8,2816]{2,1,0:T(8,128)(2,1)S(1)}, u32[]{:S(2)}, u32[]{:S(2)}) async-start(bf16[64,8,2816]{2,1,0:T(8,128)(2,1)} %bitcast.26), calls=%async_computation.2 | async-start | bytes 5767168 | tf_op jit(solution)/shard_map/all_to_all | solution.py:288
  97.9 1.9 %copy-done.10 = bf16[1,2048,768]{2,1,0:T(8,128)(2,1)S(1)} copy-done((bf16[1,2048,768]{2,1,0:T(8,128)(2,1)S(1)}, bf16[1,2048,768]{2,1,0:T(8,128)(2,1)}, u32[]{:S(2)}) %copy-start.10) | copy-done | bytes 3145752
  99.8 1.9 %copy-done.12 = bf16[1,2048,768]{2,1,0:T(8,128)(2,1)S(1)} copy-done((bf16[1,2048,768]{2,1,0:T(8,128)(2,1)S(1)}, bf16[1,2048,768]{2,1,0:T(8,128)(2,1)}, u32[]{:S(2)}) %copy-start.12) | copy-done | bytes 3145752
  101.7 1.9 %copy-done.14 = bf16[1,2048,768]{2,1,0:T(8,128)(2,1)S(1)} copy-done((bf16[1,2048,768]{2,1,0:T(8,128)(2,1)S(1)}, bf16[1,2048,768]{2,1,0:T(8,128)(2,1)}, u32[]{:S(2)}) %copy-start.14) | copy-done | bytes 3145752
  103.6 1.6 copy-done.20
  105.2 1.6 copy-done.22
  106.8 11.4 %shard_map.149 = (bf16[512,2816]{1,0:T(8,128)(2,1)S(1)}, bf16[192,2048]{1,0:T(8,128)(2,1)S(1)}, bf16[704,768]{1,0:T(8,128)(2,1)S(1)}, bf16[704,768]{1,0:T(8,128)(2,1)S(1)}) custom-call(bf16[512,2816]{1,0:T(8,128)(2,1)} %bitcast.7.got_ref.home_ref, bf16[2048,768]{1,0:T(8,128)(2,1)S(1)} %bitcast.28, bf16[2048,768]{1,0:T(8,128)(2,1)S(1)} %bitcast.30, ...), custom_call_target="tpu_custom_call" | custom-call | flops 6643777536 | bytes 22478848 | tf_op jit(solution)/shard_map/pallas_call | solution.py:272
  118.2 1.6 copy-done.2
  123.0 1.6 copy-done
  124.5 9.5 %all-to-all-start.3 = ((bf16[64,8,2816]{2,1,0:T(8,128)(2,1)}), bf16[64,8,2816]{2,1,0:T(8,128)(2,1)S(1)}, u32[]{:S(2)}, u32[]{:S(2)}) async-start(bf16[64,8,2816]{2,1,0:T(8,128)(2,1)} %bitcast.23), calls=%async_computation.3 | async-start | bytes 5767168 | tf_op jit(solution)/shard_map/all_to_all | solution.py:288
  134.0 1.2 copy-done.16
  135.2 1.1 copy-done.18
  136.4 6.1 %shard_map.153 = (bf16[1024,768]{1,0:T(8,128)(2,1)S(1)}, bf16[1024,768]{1,0:T(8,128)(2,1)S(1)}) custom-call(s32[1]{0:T(128)} %bitcast.me_ref, bf16[512,2816]{1,0:T(8,128)(2,1)} %bitcast.7.got_ref.home_ref, bf16[192,2048]{1,0:T(8,128)(2,1)S(1)} %copy-done.18, bf16[704,768]{1,0:T(8,128)(2,1)S(1)} %copy-done.16), custom_call_target="tpu_custom_call" | custom-call | flops 2214592512 | bytes 7897092 | tf_op jit(solution)/shard_map/pallas_call | solution.py:272
  142.7 6.4 %shard_map.152 = (bf16[1024,768]{1,0:T(8,128)(2,1)S(1)}, bf16[1024,768]{1,0:T(8,128)(2,1)S(1)}, bf16[1024,768]{1,0:T(8,128)(2,1)S(1)}, bf16[1024,768]{1,0:T(8,128)(2,1)S(1)}) custom-call(s32[1]{0:T(128)} %bitcast.me_ref, bf16[512,2816]{1,0:T(8,128)(2,1)S(1)} %bitcast.25, bf16[192,2048]{1,0:T(8,128)(2,1)S(1)} %copy-done.28, bf16[704,768]{1,0:T(8,128)(2,1)S(1)} %copy-done.24, ...), custom_call_target="tpu_custom_call" | custom-call | flops 4429185024 | bytes 12124164 | tf_op jit(solution)/shard_map/pallas_call | solution.py:272
  150.0 2.1 %shard_map.150 = (bf16[128,2048]{1,0:T(8,128)(2,1)}, bf16[128,512]{1,0:T(8,128)(2,1)S(1)}, bf16[128,192]{1,0:T(8,128)(2,1)S(1)}) custom-call(f32[128,128]{1,0:T(8,128)S(1)} %copy-done.7, f32[128,128]{1,0:T(8,128)S(1)} %copy-done.8, bf16[512,2816]{1,0:T(8,128)(2,1)S(1)} %bitcast.22), custom_call_target="tpu_custom_call" | custom-call | flops 738197504 | bytes 3719168 | tf_op jit(solution)/shard_map/pallas_call | solution.py:272
  152.0 1.6 fusion.2
  153.6 1.5 fusion
  155.2 1.6 fusion.1
  156.8 5.8 %all-to-all-done.3 = bf16[64,8,2816]{2,1,0:T(8,128)(2,1)S(1)} async-done(((bf16[64,8,2816]{2,1,0:T(8,128)(2,1)}), bf16[64,8,2816]{2,1,0:T(8,128)(2,1)S(1)}, u32[]{:S(2)}, u32[]{:S(2)}) %all-to-all-start.3) | async-done | bytes 2883616 | tf_op jit(solution)/shard_map/all_to_all | solution.py:288
  162.5 1.7 %shard_map.151 = bf16[128,2048]{1,0:T(8,128)(2,1)} custom-call(bf16[128,512]{1,0:T(8,128)(2,1)S(1)} %get-tuple-element.41.home_ref, bf16[128,192]{1,0:T(8,128)(2,1)S(1)} %get-tuple-element.42.far_ones_ref, bf16[512,2816]{1,0:T(8,128)(2,1)S(1)} %bitcast.21), custom_call_target="tpu_custom_call" | custom-call | flops 369098752 | bytes 3588096 | tf_op jit(solution)/shard_map/pallas_call | solution.py:272
  (50 shorter events, 6.1 us)
Async XLA Ops:
  22.2 35.6 %copy-start.6 = (bf16[128,2048]{1,0:T(8,128)(2,1)S(1)}, bf16[128,2048]{1,0:T(8,128)(2,1)}, u32[]{:S(2)}) copy-start(bf16[128,2048]{1,0:T(8,128)(2,1)} %cot_ref) | copy-start | bytes 1572868
  22.2 35.6 %copy-start.7 = (f32[128,128]{1,0:T(8,128)S(1)}, f32[128,128]{1,0:T(8,128)}, u32[]{:S(2)}) copy-start(f32[128,128]{1,0:T(8,128)} %get-tuple-element.30.slots_ref) | copy-start | bytes 196612
  22.3 35.6 %copy-start.8 = (f32[128,128]{1,0:T(8,128)S(1)}, f32[128,128]{1,0:T(8,128)}, u32[]{:S(2)}) copy-start(f32[128,128]{1,0:T(8,128)} %get-tuple-element.31.scale_ref) | copy-start | bytes 196612
  57.8 8.4 %copy-start.3 = (bf16[64,8,2816]{2,1,0:T(8,128)(2,1)}, bf16[64,8,2816]{2,1,0:T(8,128)(2,1)S(1)}, u32[]{:S(2)}) copy-start(bf16[64,8,2816]{2,1,0:T(8,128)(2,1)S(1)} %all_to_all.46) | copy-start | bytes 8650756
  60.7 29.1 %all-to-all-start.1 = ((bf16[64,8,2816]{2,1,0:T(8,128)(2,1)}), bf16[64,8,2816]{2,1,0:T(8,128)(2,1)}, u32[]{:S(2)}, u32[]{:S(2)}) async-start(bf16[64,8,2816]{2,1,0:T(8,128)(2,1)} %bitcast.6), calls=%async_computation.1 | async-start | bytes 5767168 | tf_op jit(solution)/shard_map/all_to_all | solution.py:288
  66.3 1.9 %copy-start.9 = (bf16[1,2048,768]{2,1,0:T(8,128)(2,1)S(1)}, bf16[1,2048,768]{2,1,0:T(8,128)(2,1)}, u32[]{:S(2)}) copy-start(bf16[1,2048,768]{2,1,0:T(8,128)(2,1)} %param.19) | copy-start | bytes 9437188
  68.2 1.9 %copy-start.11 = (bf16[1,2048,768]{2,1,0:T(8,128)(2,1)S(1)}, bf16[1,2048,768]{2,1,0:T(8,128)(2,1)}, u32[]{:S(2)}) copy-start(bf16[1,2048,768]{2,1,0:T(8,128)(2,1)} %param.20) | copy-start | bytes 9437188
  70.1 1.9 %copy-start.13 = (bf16[1,2048,768]{2,1,0:T(8,128)(2,1)S(1)}, bf16[1,2048,768]{2,1,0:T(8,128)(2,1)}, u32[]{:S(2)}) copy-start(bf16[1,2048,768]{2,1,0:T(8,128)(2,1)} %param.21) | copy-start | bytes 9437188
  80.2 1.6 copy-start.5
  81.8 1.0 copy-start.15
  82.7 1.4 copy-start.19
  84.1 1.3 copy-start.21
  89.8 33.1 %all-to-all-start.2 = ((bf16[64,8,2816]{2,1,0:T(8,128)(2,1)}), bf16[64,8,2816]{2,1,0:T(8,128)(2,1)S(1)}, u32[]{:S(2)}, u32[]{:S(2)}) async-start(bf16[64,8,2816]{2,1,0:T(8,128)(2,1)} %bitcast.26), calls=%async_computation.2 | async-start | bytes 5767168 | tf_op jit(solution)/shard_map/all_to_all | solution.py:288
  97.9 1.9 %copy-start.10 = (bf16[1,2048,768]{2,1,0:T(8,128)(2,1)S(1)}, bf16[1,2048,768]{2,1,0:T(8,128)(2,1)}, u32[]{:S(2)}) copy-start(bf16[1,2048,768]{2,1,0:T(8,128)(2,1)} %param.19) | copy-start | bytes 9437188
  99.8 1.9 %copy-start.12 = (bf16[1,2048,768]{2,1,0:T(8,128)(2,1)S(1)}, bf16[1,2048,768]{2,1,0:T(8,128)(2,1)}, u32[]{:S(2)}) copy-start(bf16[1,2048,768]{2,1,0:T(8,128)(2,1)} %param.20) | copy-start | bytes 9437188
  101.7 1.9 %copy-start.14 = (bf16[1,2048,768]{2,1,0:T(8,128)(2,1)S(1)}, bf16[1,2048,768]{2,1,0:T(8,128)(2,1)}, u32[]{:S(2)}) copy-start(bf16[1,2048,768]{2,1,0:T(8,128)(2,1)} %param.21) | copy-start | bytes 9437188
  103.6 1.6 copy-start.20
  105.2 1.6 copy-start.22
  118.2 1.6 copy-start.2
  120.7 1.0 copy-start.23
  123.0 1.6 copy-start
  124.5 38.0 %all-to-all-start.3 = ((bf16[64,8,2816]{2,1,0:T(8,128)(2,1)}), bf16[64,8,2816]{2,1,0:T(8,128)(2,1)S(1)}, u32[]{:S(2)}, u32[]{:S(2)}) async-start(bf16[64,8,2816]{2,1,0:T(8,128)(2,1)} %bitcast.23), calls=%async_computation.3 | async-start | bytes 5767168 | tf_op jit(solution)/shard_map/all_to_all | solution.py:288
  134.0 1.2 copy-start.16
  135.2 1.1 copy-start.18
  136.4 6.2 %copy-start.4 = (bf16[64,8,2816]{2,1,0:T(8,128)(2,1)S(1)}, bf16[64,8,2816]{2,1,0:T(8,128)(2,1)}, u32[]{:S(2)}) copy-start(bf16[64,8,2816]{2,1,0:T(8,128)(2,1)} %copy-done.3) | copy-start | bytes 8650756
  136.4 6.3 %copy-start.24 = (bf16[704,768]{1,0:T(8,128)(2,1)S(1)}, bf16[704,768]{1,0:T(8,128)(2,1)}, u32[]{:S(2)}) copy-start(bf16[704,768]{1,0:T(8,128)(2,1)} %copy-done.23) | copy-start | bytes 3244036
  136.4 6.3 %copy-start.26 = (bf16[704,768]{1,0:T(8,128)(2,1)S(1)}, bf16[704,768]{1,0:T(8,128)(2,1)}, u32[]{:S(2)}) copy-start(bf16[704,768]{1,0:T(8,128)(2,1)} %copy-done.25) | copy-start | bytes 3244036
  136.4 6.3 %copy-start.28 = (bf16[192,2048]{1,0:T(8,128)(2,1)S(1)}, bf16[192,2048]{1,0:T(8,128)(2,1)}, u32[]{:S(2)}) copy-start(bf16[192,2048]{1,0:T(8,128)(2,1)} %copy-done.27) | copy-start | bytes 2359300
  142.5 9.5 %collective-permute-start.2 = (bf16[1024,768]{1,0:T(8,128)(2,1)S(1)}, bf16[1024,768]{1,0:T(8,128)(2,1)S(1)}, u32[]{:S(2)}, u32[]{:S(2)}) collective-permute-start(bf16[1024,768]{1,0:T(8,128)(2,1)S(1)} %get-tuple-element.54), channel_id=1, source_target_pairs={{0,64},{64,0},{1,65},{65,1},{2,66},{66,2},{3,67},{67,3},{4,68},{68... | collective-permute-start | bytes 4718600 | tf_op jit(solution)/shard_map/ppermute | solution.py:344
  142.7 7.3 %copy-start.1 = (bf16[64,8,2816]{2,1,0:T(8,128)(2,1)S(1)}, bf16[64,8,2816]{2,1,0:T(8,128)(2,1)}, u32[]{:S(2)}) copy-start(bf16[64,8,2816]{2,1,0:T(8,128)(2,1)} %copy-done) | copy-start | bytes 8650756
  149.1 4.5 %collective-permute-start = (bf16[1024,768]{1,0:T(8,128)(2,1)S(1)}, bf16[1024,768]{1,0:T(8,128)(2,1)S(1)}, u32[]{:S(2)}, u32[]{:S(2)}) collective-permute-start(bf16[1024,768]{1,0:T(8,128)(2,1)S(1)} %get-tuple-element.48), channel_id=1, source_target_pairs={{0,64},{64,0},{1,65},{65,1},{2,66},{66,2},{3,67},{67,3},{4,68},{68... | collective-permute-start | bytes 4718600 | tf_op jit(solution)/shard_map/ppermute | solution.py:344
  149.6 5.5 %collective-permute-start.1 = (bf16[1024,768]{1,0:T(8,128)(2,1)S(1)}, bf16[1024,768]{1,0:T(8,128)(2,1)S(1)}, u32[]{:S(2)}, u32[]{:S(2)}) collective-permute-start(bf16[1024,768]{1,0:T(8,128)(2,1)S(1)} %get-tuple-element.50), channel_id=1, source_target_pairs={{0,64},{64,0},{1,65},{65,1},{2,66},{66,2},{3,67},{67,3},{4,68},{68... | collective-permute-start | bytes 4718600 | tf_op jit(solution)/shard_map/ppermute | solution.py:344
  (3 other events, 2.8 us)

commit v5 on v4

--- a/solution.py
+++ b/solution.py
@@ -23,7 +23,7 @@
 GROUP = 32
 HALF = D // 2
 STEP = 256
-LATER = 810
+LATER = 820
 BF = jnp.bfloat16
 F32 = jnp.float32
 TURN = ((0,), (0,))
@@ -239,7 +239,12 @@
         lax.fori_loop(0, HALF // STEP, step, 0)
 
 
-def mixed_kernel(slots_ref, scale_ref, got_ref, mixed_ref, home_ones_ref, far_ones_ref, far_ref):
+def ones_kernel(slots_ref, home_ones_ref, far_ones_ref):
+    home_ones_ref[...] = home_picks(slots_ref[...]).T.astype(BF)
+    far_ones_ref[...] = far_picks(slots_ref[...]).T.astype(BF)
+
+
+def mixed_kernel(slots_ref, scale_ref, got_ref, mixed_ref, far_ref):
     unfold(got_ref[:, D:], far_ref)
     slots, scale = slots_ref[...], scale_ref[...]
     home = jnp.concatenate(split(home_picks(slots, scale)), axis=1)
@@ -248,8 +253,6 @@
         cols = slice(c, c + STEP)
         both = dot(home, got_ref[:, cols], TURN) + dot(far, far_ref[:, cols], TURN)
         mixed_ref[:, cols] = (both[:TOK] + both[TOK:]).astype(BF)
-    home_ones_ref[...] = home_picks(slots).T.astype(BF)
-    far_ones_ref[...] = far_picks(slots).T.astype(BF)
 
 
 def back_kernel(home_ref, far_ones_ref, got_ref, grad_ref, far_ref):
@@ -323,10 +326,15 @@
     send_out, far_x, hidden, gate_factor, up_factor = call(
         forward_kernel, [packed, far, act, act32, act32], (got_x, gate, up, down), 3 * product
     )
+    slots_later, got_g = lax.optimization_barrier((slots, got_g))
+    home_ones, far_ones = call(
+        ones_kernel, [shape(TOK, HOME), shape(TOK, FAR)], (slots_later,), move // 16, limit=16
+    )
+    send_out, home_ones = lax.optimization_barrier((send_out, home_ones))
     got_out = exchange(send_out)
     send_back, far_g, back_gate, back_up = call(
         backward_kernel, [packed, far, act, act],
-        (got_g, gate, up, down, gate_factor, up_factor), 3 * product,
+        (got_g, gate, up, down, gate_factor, up_factor), 3 * product, limit=60,
     )
     send_back, got_out = lax.optimization_barrier((send_back, got_out))
     got_back = exchange(send_back)
@@ -344,8 +352,8 @@
         (keep.astype(F32) + lax.ppermute(sent, "dp", ((0, 1), (1, 0))).astype(F32)).astype(BF)[None]
         for sent, keep in ((send_gate, keep_gate), (send_up, keep_up), (send_down, keep_down))
     ]
-    mixed, home_ones, far_ones = call(
-        mixed_kernel, [shape(TOK, D), shape(TOK, HOME), shape(TOK, FAR)], (slots, scale, got_out),
+    (mixed,) = call(
+        mixed_kernel, [shape(TOK, D)], (slots, scale, got_out),
         2 * move, [far_scratch], 16,
     )
     (grad_tokens,) = call(

time: 165 us -> 166 us (level)
  local copies, waits for them, and re-layouts: 29.1 us -> 14.2 us
  waiting for transfers between devices: 9.58 us -> 22.5 us
  Pallas kernels: 60.3 us -> 68.3 us
  starting transfers between devices: 24.1 us -> 18.7 us
    unnamed x58 -> x36, local copies, waits for them, and re-layouts: 29.1 us -> 14.2 us
    all_to_all x3, waiting for transfers between devices: 9.58 us -> 20.7 us  [exchange(): lax.all_to_all(values, 'expert', split_axis=0, concat_axis=0, tiled=True)]
    pallas_call x8 -> x9, Pallas kernels: 60.3 us -> 68.3 us  [call(): pl.pallas_call(kernel, out_shape=outs, in_specs=in_specs or [VMEM] * len(...]
    all_to_all x3, starting transfers between devices: 23.1 us -> 17.8 us  [exchange(): lax.all_to_all(values, 'expert', split_axis=0, concat_axis=0, tiled=True)]
    ppermute x3, waiting for transfers between devices: 0.01 us -> 1.77 us  [shards(): lax.ppermute(sent, 'dp', ((0, 1), (1, 0))).astype(F32)]
  transfers between devices with their start and end apart: 6 -> 6, of which waited for: 3 -> 5; matrix products, arithmetic and copies ran while one was open for 3% -> 3% of each run, Pallas kernels for 21% -> 24%
where the time goes in v5:
time: 166 us; the launch traced here: 165 us
  Pallas kernels  68.3 us (41%)
  blocking collectives  35.8 us (22%)
  waiting for transfers between devices  22.5 us (14%)
  starting transfers between devices  18.7 us (11%)
  local copies, waits for them, and re-layouts  14.2 us (9%)
  other arithmetic  4.8 us (3%)
    pallas_call x9, Pallas kernels, call(): pl.pallas_call(kernel, out_shape=outs, in_specs=in_specs or [VMEM] * len(...  68.3 us
    all_to_all x1, blocking collectives, exchange(): lax.all_to_all(values, 'expert', split_axis=0, concat_axis=0, tiled=True)  35.8 us
    all_to_all x3, waiting for transfers between devices, exchange(): lax.all_to_all(values, 'expert', split_axis=0, concat_axis=0, tiled=True)  20.7 us
    all_to_all x3, starting transfers between devices, exchange(): lax.all_to_all(values, 'expert', split_axis=0, concat_axis=0, tiled=True)  17.8 us
    unnamed x36, local copies, waits for them, and re-layouts  14.2 us
    broadcast_in_dim x3, other arithmetic, shards(): (keep.astype(F32) + lax.ppermute(sent, 'dp', ((0, 1), (1, 0))).astype(F32...  4.8 us
  transfers between devices with their start and end apart: 6, of which 5 were waited for; matrix products, arithmetic and copies ran while one was open for 3% of the time, Pallas kernels for 24%

profile of v5, /device:TPU:1, one launch (start us, length us, event | category | flops | bytes accessed | tf_op | source)
XLA Modules:
  0.0 165.1 jit_solution(4661397141878523295)
XLA Ops:
  0.6 21.8 %shard_map.146 = (bf16[512,2816]{1,0:T(8,128)(2,1)}, f32[128,128]{1,0:T(8,128)}, f32[128,128]{1,0:T(8,128)}) custom-call(s32[1]{0:T(128)} %bitcast.me_ref, s32[8]{0:T(128)} %hot_hbm.1, s32[8]{0:T(128)} %holder_hbm.1, s32[64]{0:T(128)} %cap_hbm.1, s32[8,128]{1,0:T(8,128)} %bitcast.33, s32[8,128]{1,0:T(8,128)} %bitcast.34, s32[8,128]{1,0:T(8,128)} %bitcast.35, ...), custom_call_target="tpu_custom_call" | custom-call | flops 369098752 | bytes 3551556 | tf_op jit(solution)/shard_map/pallas_call | solution.py:275
  22.5 35.8 %all_to_all.47 = bf16[64,8,2816]{2,1,0:T(8,128)(2,1)S(1)} all-to-all(bf16[64,8,2816]{2,1,0:T(8,128)(2,1)} %bitcast.32), channel_id=1, replica_groups=mesh['dp'=2,'expert'=64] {'expert'}, dimensions={0} | all-to-all | bytes 5767168 | tf_op jit(solution)/shard_map/all_to_all | solution.py:291
  58.3 2.9 %shard_map.147 = bf16[512,2816]{1,0:T(8,128)(2,1)} custom-call(f32[128,128]{1,0:T(8,128)S(1)} %copy-done.4, f32[128,128]{1,0:T(8,128)S(1)} %copy-done.5, bf16[128,2048]{1,0:T(8,128)(2,1)S(1)} %copy-done.3), custom_call_target="tpu_custom_call" | custom-call | flops 738197504 | bytes 3538944 | tf_op jit(solution)/shard_map/pallas_call | solution.py:275
  61.2 5.6 %all-to-all-start.1 = ((bf16[64,8,2816]{2,1,0:T(8,128)(2,1)}), bf16[64,8,2816]{2,1,0:T(8,128)(2,1)}, u32[]{:S(2)}, u32[]{:S(2)}) async-start(bf16[64,8,2816]{2,1,0:T(8,128)(2,1)} %bitcast.6), calls=%async_computation.1 | async-start | bytes 5767168 | tf_op jit(solution)/shard_map/all_to_all | solution.py:291
  66.8 1.9 %copy-done.6 = bf16[1,2048,768]{2,1,0:T(8,128)(2,1)S(1)} copy-done((bf16[1,2048,768]{2,1,0:T(8,128)(2,1)S(1)}, bf16[1,2048,768]{2,1,0:T(8,128)(2,1)}, u32[]{:S(2)}) %copy-start.6) | copy-done | bytes 3145752
  68.6 1.9 %copy-done.7 = bf16[1,2048,768]{2,1,0:T(8,128)(2,1)S(1)} copy-done((bf16[1,2048,768]{2,1,0:T(8,128)(2,1)S(1)}, bf16[1,2048,768]{2,1,0:T(8,128)(2,1)}, u32[]{:S(2)}) %copy-start.7) | copy-done | bytes 3145752
  70.5 1.9 %copy-done.8 = bf16[1,2048,768]{2,1,0:T(8,128)(2,1)S(1)} copy-done((bf16[1,2048,768]{2,1,0:T(8,128)(2,1)S(1)}, bf16[1,2048,768]{2,1,0:T(8,128)(2,1)}, u32[]{:S(2)}) %copy-start.8) | copy-done | bytes 3145752
  72.4 8.2 %shard_map.148 = (bf16[512,2816]{1,0:T(8,128)(2,1)S(1)}, bf16[192,2048]{1,0:T(8,128)(2,1)S(1)}, bf16[704,768]{1,0:T(8,128)(2,1)S(1)}, f32[704,768]{1,0:T(8,128)S(1)}, f32[704,768]{1,0:T(8,128)S(1)}) custom-call(bf16[512,2816]{1,0:T(8,128)(2,1)S(1)} %bitcast.22, bf16[2048,768]{1,0:T(8,128)(2,1)S(1)} %bitcast.26, bf16[2048,768]{1,0:T(8,128)(2,1)S(1)} %bitcast.28, ...), custom_call_target="tpu_custom_call" | custom-call | flops 6643777536 | bytes 21397504 | tf_op jit(solution)/shard_map/pallas_call | solution.py:275
  80.7 1.5 copy-done.2
  82.2 1.0 copy-done.9
  83.2 1.4 copy-done.12
  84.6 1.3 copy-done.13
  86.0 0.9 copy-done.16
  86.8 3.1 %all-to-all-done.1 = bf16[64,8,2816]{2,1,0:T(8,128)(2,1)} async-done(((bf16[64,8,2816]{2,1,0:T(8,128)(2,1)}), bf16[64,8,2816]{2,1,0:T(8,128)(2,1)}, u32[]{:S(2)}, u32[]{:S(2)}) %all-to-all-start.1) | async-done | bytes 2883616 | tf_op jit(solution)/shard_map/all_to_all | solution.py:291
  90.1 6.6 %all-to-all-start.2 = ((bf16[64,8,2816]{2,1,0:T(8,128)(2,1)}), bf16[64,8,2816]{2,1,0:T(8,128)(2,1)S(1)}, u32[]{:S(2)}, u32[]{:S(2)}) async-start(bf16[64,8,2816]{2,1,0:T(8,128)(2,1)} %bitcast.24), calls=%async_computation.2 | async-start | bytes 5767168 | tf_op jit(solution)/shard_map/all_to_all | solution.py:291
  96.8 17.0 %shard_map.149 = (bf16[512,2816]{1,0:T(8,128)(2,1)}, bf16[192,2048]{1,0:T(8,128)(2,1)}, bf16[704,768]{1,0:T(8,128)(2,1)}, bf16[704,768]{1,0:T(8,128)(2,1)}) custom-call(bf16[512,2816]{1,0:T(8,128)(2,1)} %bitcast.7.got_ref.home_ref, bf16[2048,768]{1,0:T(8,128)(2,1)} %bitcast.25, bf16[2048,768]{1,0:T(8,128)(2,1)} %bitcast.27, bf16[2048,768]{1,0:T(8,128)(2,1)} %bitcast.29, ...), custom_call_target="tpu_custom_call" | custom-call | flops 6643777536 | bytes 22478848 | tf_op jit(solution)/shard_map/pallas_call | solution.py:275
  113.7 9.7 %all-to-all-done.2 = bf16[64,8,2816]{2,1,0:T(8,128)(2,1)S(1)} async-done(((bf16[64,8,2816]{2,1,0:T(8,128)(2,1)}), bf16[64,8,2816]{2,1,0:T(8,128)(2,1)S(1)}, u32[]{:S(2)}, u32[]{:S(2)}) %all-to-all-start.2) | async-done | bytes 2883616 | tf_op jit(solution)/shard_map/all_to_all | solution.py:291
  123.5 5.6 %all-to-all-start.3 = ((bf16[64,8,2816]{2,1,0:T(8,128)(2,1)}), bf16[64,8,2816]{2,1,0:T(8,128)(2,1)}, u32[]{:S(2)}, u32[]{:S(2)}) async-start(bf16[64,8,2816]{2,1,0:T(8,128)(2,1)} %bitcast.31), calls=%async_computation.3 | async-start | bytes 5767168 | tf_op jit(solution)/shard_map/all_to_all | solution.py:291
  129.1 1.2 copy-done.10
  130.3 1.1 copy-done.11
  131.4 6.1 %shard_map.154 = (bf16[1024,768]{1,0:T(8,128)(2,1)S(1)}, bf16[1024,768]{1,0:T(8,128)(2,1)S(1)}) custom-call(s32[1]{0:T(128)} %bitcast.me_ref, bf16[512,2816]{1,0:T(8,128)(2,1)} %bitcast.7.got_ref.home_ref, bf16[192,2048]{1,0:T(8,128)(2,1)S(1)} %copy-done.11, bf16[704,768]{1,0:T(8,128)(2,1)S(1)} %copy-done.10), custom_call_target="tpu_custom_call" | custom-call | flops 2214592512 | bytes 7897092 | tf_op jit(solution)/shard_map/pallas_call | solution.py:275
  137.7 6.5 %shard_map.153 = (bf16[1024,768]{1,0:T(8,128)(2,1)S(1)}, bf16[1024,768]{1,0:T(8,128)(2,1)S(1)}, bf16[1024,768]{1,0:T(8,128)(2,1)S(1)}, bf16[1024,768]{1,0:T(8,128)(2,1)S(1)}) custom-call(s32[1]{0:T(128)} %bitcast.me_ref, bf16[512,2816]{1,0:T(8,128)(2,1)S(1)} %bitcast.23, bf16[192,2048]{1,0:T(8,128)(2,1)S(1)} %copy-done.17, bf16[704,768]{1,0:T(8,128)(2,1)S(1)} %copy-done.14, ...), custom_call_target="tpu_custom_call" | custom-call | flops 4429185024 | bytes 12124164 | tf_op jit(solution)/shard_map/pallas_call | solution.py:275
  144.2 0.6 collective-permute-start.1
  144.7 0.3 collective-permute-start
  145.1 1.6 fusion.2
  146.7 1.1 collective-permute-done.1
  147.8 1.6 fusion.1
  149.4 0.6 collective-permute-done
  150.0 1.6 fusion
  151.6 2.1 %shard_map.151 = bf16[128,2048]{1,0:T(8,128)(2,1)} custom-call(f32[128,128]{1,0:T(8,128)S(1)} %copy-done.4, f32[128,128]{1,0:T(8,128)S(1)} %copy-done.5, bf16[512,2816]{1,0:T(8,128)(2,1)S(1)} %bitcast.21), custom_call_target="tpu_custom_call" | custom-call | flops 738197504 | bytes 3538944 | tf_op jit(solution)/shard_map/pallas_call | solution.py:275
  153.7 7.9 %all-to-all-done.3 = bf16[64,8,2816]{2,1,0:T(8,128)(2,1)} async-done(((bf16[64,8,2816]{2,1,0:T(8,128)(2,1)}), bf16[64,8,2816]{2,1,0:T(8,128)(2,1)}, u32[]{:S(2)}, u32[]{:S(2)}) %all-to-all-start.3) | async-done | bytes 2883616 | tf_op jit(solution)/shard_map/all_to_all | solution.py:291
  161.6 3.5 %shard_map.152 = bf16[128,2048]{1,0:T(8,128)(2,1)} custom-call(bf16[128,512]{1,0:T(8,128)(2,1)S(1)} %get-tuple-element.47.home_ref, bf16[128,192]{1,0:T(8,128)(2,1)S(1)} %get-tuple-element.48.far_ones_ref, bf16[512,2816]{1,0:T(8,128)(2,1)} %bitcast.14.got_ref), custom_call_target="tpu_custom_call" | custom-call | flops 369098752 | bytes 3588096 | tf_op jit(solution)/shard_map/pallas_call | solution.py:275
  (29 shorter events, 0.3 us)
Async XLA Ops:
  22.5 35.8 %copy-start.3 = (bf16[128,2048]{1,0:T(8,128)(2,1)S(1)}, bf16[128,2048]{1,0:T(8,128)(2,1)}, u32[]{:S(2)}) copy-start(bf16[128,2048]{1,0:T(8,128)(2,1)} %cot_ref) | copy-start | bytes 1572868
  22.5 35.8 %copy-start.4 = (f32[128,128]{1,0:T(8,128)S(1)}, f32[128,128]{1,0:T(8,128)}, u32[]{:S(2)}) copy-start(f32[128,128]{1,0:T(8,128)} %get-tuple-element.43.slots_ref) | copy-start | bytes 196612
  22.5 35.8 %copy-start.5 = (f32[128,128]{1,0:T(8,128)S(1)}, f32[128,128]{1,0:T(8,128)}, u32[]{:S(2)}) copy-start(f32[128,128]{1,0:T(8,128)} %get-tuple-element.34.scale_ref) | copy-start | bytes 196612
  58.3 8.5 %copy-start = (bf16[64,8,2816]{2,1,0:T(8,128)(2,1)}, bf16[64,8,2816]{2,1,0:T(8,128)(2,1)S(1)}, u32[]{:S(2)}) copy-start(bf16[64,8,2816]{2,1,0:T(8,128)(2,1)S(1)} %all_to_all.47) | copy-start | bytes 8650756
  61.2 28.8 %all-to-all-start.1 = ((bf16[64,8,2816]{2,1,0:T(8,128)(2,1)}), bf16[64,8,2816]{2,1,0:T(8,128)(2,1)}, u32[]{:S(2)}, u32[]{:S(2)}) async-start(bf16[64,8,2816]{2,1,0:T(8,128)(2,1)} %bitcast.6), calls=%async_computation.1 | async-start | bytes 5767168 | tf_op jit(solution)/shard_map/all_to_all | solution.py:291
  66.8 1.9 %copy-start.6 = (bf16[1,2048,768]{2,1,0:T(8,128)(2,1)S(1)}, bf16[1,2048,768]{2,1,0:T(8,128)(2,1)}, u32[]{:S(2)}) copy-start(bf16[1,2048,768]{2,1,0:T(8,128)(2,1)} %param.19) | copy-start | bytes 9437188
  68.6 1.9 %copy-start.7 = (bf16[1,2048,768]{2,1,0:T(8,128)(2,1)S(1)}, bf16[1,2048,768]{2,1,0:T(8,128)(2,1)}, u32[]{:S(2)}) copy-start(bf16[1,2048,768]{2,1,0:T(8,128)(2,1)} %param.20) | copy-start | bytes 9437188
  70.5 1.9 %copy-start.8 = (bf16[1,2048,768]{2,1,0:T(8,128)(2,1)S(1)}, bf16[1,2048,768]{2,1,0:T(8,128)(2,1)}, u32[]{:S(2)}) copy-start(bf16[1,2048,768]{2,1,0:T(8,128)(2,1)} %param.21) | copy-start | bytes 9437188
  80.7 1.6 copy-start.2
  82.2 1.0 copy-start.9
  83.2 1.4 copy-start.12
  84.6 1.3 copy-start.13
  86.0 0.9 copy-start.16
  90.1 33.4 %all-to-all-start.2 = ((bf16[64,8,2816]{2,1,0:T(8,128)(2,1)}), bf16[64,8,2816]{2,1,0:T(8,128)(2,1)S(1)}, u32[]{:S(2)}, u32[]{:S(2)}) async-start(bf16[64,8,2816]{2,1,0:T(8,128)(2,1)} %bitcast.24), calls=%async_computation.2 | async-start | bytes 5767168 | tf_op jit(solution)/shard_map/all_to_all | solution.py:291
  123.5 38.1 %all-to-all-start.3 = ((bf16[64,8,2816]{2,1,0:T(8,128)(2,1)}), bf16[64,8,2816]{2,1,0:T(8,128)(2,1)}, u32[]{:S(2)}, u32[]{:S(2)}) async-start(bf16[64,8,2816]{2,1,0:T(8,128)(2,1)} %bitcast.31), calls=%async_computation.3 | async-start | bytes 5767168 | tf_op jit(solution)/shard_map/all_to_all | solution.py:291
  129.0 1.2 copy-start.10
  130.3 1.1 copy-start.11
  131.4 6.3 %copy-start.1 = (bf16[64,8,2816]{2,1,0:T(8,128)(2,1)S(1)}, bf16[64,8,2816]{2,1,0:T(8,128)(2,1)}, u32[]{:S(2)}) copy-start(bf16[64,8,2816]{2,1,0:T(8,128)(2,1)} %copy-done) | copy-start | bytes 8650756
  131.4 6.3 %copy-start.14 = (bf16[704,768]{1,0:T(8,128)(2,1)S(1)}, bf16[704,768]{1,0:T(8,128)(2,1)}, u32[]{:S(2)}) copy-start(bf16[704,768]{1,0:T(8,128)(2,1)} %get-tuple-element.51.refs_0_) | copy-start | bytes 3244036
  131.4 6.3 %copy-start.15 = (bf16[704,768]{1,0:T(8,128)(2,1)S(1)}, bf16[704,768]{1,0:T(8,128)(2,1)}, u32[]{:S(2)}) copy-start(bf16[704,768]{1,0:T(8,128)(2,1)} %get-tuple-element.52.refs_1_) | copy-start | bytes 3244036
  131.4 6.3 %copy-start.17 = (bf16[192,2048]{1,0:T(8,128)(2,1)S(1)}, bf16[192,2048]{1,0:T(8,128)(2,1)}, u32[]{:S(2)}) copy-start(bf16[192,2048]{1,0:T(8,128)(2,1)} %copy-done.16) | copy-start | bytes 2359300
  137.6 7.5 %collective-permute-start.2 = (bf16[1024,768]{1,0:T(8,128)(2,1)S(1)}, bf16[1024,768]{1,0:T(8,128)(2,1)S(1)}, u32[]{:S(2)}, u32[]{:S(2)}) collective-permute-start(bf16[1024,768]{1,0:T(8,128)(2,1)S(1)} %get-tuple-element.60), channel_id=1, source_target_pairs={{0,64},{64,0},{1,65},{65,1},{2,66},{66,2},{3,67},{67,3},{4,68},{68... | collective-permute-start | bytes 4718600 | tf_op jit(solution)/shard_map/ppermute | solution.py:352
  144.2 3.6 %collective-permute-start.1 = (bf16[1024,768]{1,0:T(8,128)(2,1)S(1)}, bf16[1024,768]{1,0:T(8,128)(2,1)S(1)}, u32[]{:S(2)}, u32[]{:S(2)}) collective-permute-start(bf16[1024,768]{1,0:T(8,128)(2,1)S(1)} %get-tuple-element.56), channel_id=1, source_target_pairs={{0,64},{64,0},{1,65},{65,1},{2,66},{66,2},{3,67},{67,3},{4,68},{68... | collective-permute-start | bytes 4718600 | tf_op jit(solution)/shard_map/ppermute | solution.py:352
  144.7 5.3 %collective-permute-start = (bf16[1024,768]{1,0:T(8,128)(2,1)S(1)}, bf16[1024,768]{1,0:T(8,128)(2,1)S(1)}, u32[]{:S(2)}, u32[]{:S(2)}) collective-permute-start(bf16[1024,768]{1,0:T(8,128)(2,1)S(1)} %get-tuple-element.54), channel_id=1, source_target_pairs={{0,64},{64,0},{1,65},{65,1},{2,66},{66,2},{3,67},{67,3},{4,68},{68... | collective-permute-start | bytes 4718600 | tf_op jit(solution)/shard_map/ppermute | solution.py:352
